TPU v7x, 512 devices: a whole 4x8x8 slice. The times are simulated.
512 devices in a mesh: ctx: 16 (over z_hi, x, core), dp: 32 (over z_lo, y).
Axes of the slice: x: 4, y: 8, z: 8 (z_hi: 2, z_lo: 4; z = z_hi * 4 + z_lo), core: 2. Of those that a mesh axis runs over, the one named last changes fastest.
Arguments:
- upstream: bfloat16 [4096, 2, 4096], P('ctx', None, 'dp'), may hold values from -6 to 6
- gate_value: bfloat16 [4096, 2, 4096], P('ctx', None, 'dp'), may hold values from -2 to 2
- conv_input: bfloat16 [4096, 2, 4096], P('ctx', None, 'dp'), may hold values from -2 to 2
- filters: float32 [32, 128, 4096], P(None, 'ctx', 'dp'), may hold values from -1 to 1
- skip_gain: float32 [4096], P('dp'), may hold values from 0.25 to 2
Outputs:
- input_grad: bfloat16 [4096, 2, 4096], P('ctx', None, 'dp')
- filter_grad: float32 [32, 128, 4096], P(None, 'ctx', 'dp')
All inputs are finite; a program needn't handle non-finite values.
Results may differ from a plain program's by a relative error of at most 0.0049.
Values may be sent and summed in bfloat16 or wider, within the bound.
A program may use at most 64 MiB of HBM per device.

v0:
```python
import math

import jax
import jax.numpy as jnp
from jax import lax
from jax.sharding import PartitionSpec as P

RADIX = 128


precise = lax.Precision.HIGHEST


def dft_tables(padded, inner_size):
    outer = padded // inner_size
    half_rows = outer // 2
    upper = inner_size // 2 + 1
    freq_low = jnp.arange(outer, dtype=jnp.int32)
    row_index = jnp.arange(half_rows, dtype=jnp.int32)
    inner_index = jnp.arange(inner_size, dtype=jnp.int32)
    freq_high = jnp.arange(upper, dtype=jnp.int32)
    angle_rows = (freq_low[:, None] * row_index[None, :] % outer).astype(jnp.float32) * (
        2.0 * math.pi / outer
    )
    angle_twist = (freq_low[:, None] * inner_index[None, :] % padded).astype(jnp.float32) * (
        2.0 * math.pi / padded
    )
    angle_inner = (inner_index[:, None] * freq_high[None, :] % inner_size).astype(jnp.float32) * (
        2.0 * math.pi / inner_size
    )
    frequency = freq_low[:, None] + outer * freq_high[None, :]
    middle = padded // 2
    edge = (frequency == 0) | (frequency == middle)
    weights = jnp.where(edge, 0.5, jnp.where(frequency < middle, 1.0, 0.0)) * (2.0 / padded)
    return (
        jnp.cos(angle_rows),
        -jnp.sin(angle_rows),
        jnp.cos(angle_twist),
        -jnp.sin(angle_twist),
        jnp.cos(angle_inner),
        -jnp.sin(angle_inner),
        weights.astype(jnp.float32),
    )


def spectrum(signal, tables):
    cos_rows, sin_rows, cos_twist, sin_twist, cos_inner, sin_inner, weights = tables
    half_rows = cos_rows.shape[1]
    inner_size = cos_inner.shape[0]
    columns = signal.shape[1]
    blocks = signal.astype(jnp.float32).reshape(half_rows, inner_size, columns)
    first_real = jnp.einsum("kb,bac->kac", cos_rows, blocks, precision=precise)
    first_imag = jnp.einsum("kb,bac->kac", sin_rows, blocks, precision=precise)
    twist_real = cos_twist[:, :, None]
    twist_imag = sin_twist[:, :, None]
    turned_real = first_real * twist_real - first_imag * twist_imag
    turned_imag = first_real * twist_imag + first_imag * twist_real
    out_real = jnp.einsum("kac,ae->kec", turned_real, cos_inner, precision=precise) - jnp.einsum(
        "kac,ae->kec", turned_imag, sin_inner, precision=precise
    )
    out_imag = jnp.einsum("kac,ae->kec", turned_real, sin_inner, precision=precise) + jnp.einsum(
        "kac,ae->kec", turned_imag, cos_inner, precision=precise
    )
    return (out_real, out_imag)


def real_inverse(spec_real, spec_imag, tables):
    cos_rows, sin_rows, cos_twist, sin_twist, cos_inner, sin_inner, weights = tables
    half_rows = cos_rows.shape[1]
    inner_size = cos_inner.shape[0]
    columns = spec_real.shape[2]
    spec_real = spec_real * weights[:, :, None]
    spec_imag = spec_imag * weights[:, :, None]
    back_real = jnp.einsum("kec,ae->kac", spec_real, cos_inner, precision=precise) + jnp.einsum(
        "kec,ae->kac", spec_imag, sin_inner, precision=precise
    )
    back_imag = jnp.einsum("kec,ae->kac", spec_imag, cos_inner, precision=precise) - jnp.einsum(
        "kec,ae->kac", spec_real, sin_inner, precision=precise
    )
    twist_real = cos_twist[:, :, None]
    twist_imag = sin_twist[:, :, None]
    untwist_real = back_real * twist_real + back_imag * twist_imag
    untwist_imag = back_imag * twist_real - back_real * twist_imag
    time_rows = jnp.einsum("kb,kac->bac", cos_rows, untwist_real, precision=precise) + jnp.einsum(
        "kb,kac->bac", sin_rows, untwist_imag, precision=precise
    )
    return time_rows.reshape(half_rows * inner_size, columns)


def times_conj(left_real, left_imag, right_real, right_imag):
    return (
        left_real * right_real + left_imag * right_imag,
        left_imag * right_real - left_real * right_imag,
    )


def correlate(grad_cols, input_cols, filt_real, filt_imag, gain_cols, tables):
    grad_real, grad_imag = spectrum(grad_cols, tables)
    input_real, input_imag = spectrum(input_cols, tables)
    prod_real, prod_imag = times_conj(grad_real, grad_imag, filt_real, filt_imag)
    back_sum = real_inverse(prod_real, prod_imag, tables)
    output_cols = back_sum + gain_cols[None, :] * grad_cols.astype(jnp.float32)
    cross_real, cross_imag = times_conj(grad_real, grad_imag, input_real, input_imag)
    return (output_cols, cross_real, cross_imag)


def body(upstream, gate_value, conv_input, filters, skip_gain):
    tokens = upstream.shape[0]
    seq_count = upstream.shape[1]
    ctx_count = lax.axis_size("ctx")
    seqlen = tokens * ctx_count
    tables = dft_tables(2 * seqlen, RADIX)
    gate_grad = (upstream.astype(jnp.float32) * gate_value.astype(jnp.float32)).astype(jnp.bfloat16)
    grads_here, inputs_here = (
        lax.all_to_all(gate_grad, "ctx", split_axis=2, concat_axis=0, tiled=True),
        lax.all_to_all(conv_input, "ctx", split_axis=2, concat_axis=0, tiled=True),
    )
    own_width = grads_here.shape[2]
    grad_cols = grads_here.reshape(seqlen, seq_count * own_width)
    input_cols = inputs_here.reshape(seqlen, seq_count * own_width)
    whole_filters = lax.all_to_all(filters, "dp", split_axis=0, concat_axis=2, tiled=True)
    own_real, own_imag = spectrum(whole_filters[0].T, tables)
    filt_real = jnp.tile(own_real, (1, 1, seq_count))
    filt_imag = jnp.tile(own_imag, (1, 1, seq_count))
    own_gain = lax.dynamic_slice_in_dim(skip_gain, lax.axis_index("ctx") * own_width, own_width)
    gain_cols = jnp.tile(own_gain, seq_count)
    output_cols, cross_real, cross_imag = correlate(
        grad_cols, input_cols, filt_real, filt_imag, gain_cols, tables
    )
    lag_rows = (
        real_inverse(cross_real, cross_imag, tables)
        .reshape(seqlen, seq_count, own_width)
        .sum(axis=1)
    )
    lag_grad = (lag_rows / seq_count).T[None, :, :]
    filter_grad = lax.all_to_all(lag_grad, "dp", split_axis=2, concat_axis=0, tiled=True)
    spread = output_cols.astype(jnp.bfloat16).reshape(seqlen, seq_count, own_width)
    input_grad = lax.all_to_all(spread, "ctx", split_axis=0, concat_axis=2, tiled=True)
    return (input_grad, filter_grad)


def solution(mesh):
    in_specs = (
        P("ctx", None, "dp"),
        P("ctx", None, "dp"),
        P("ctx", None, "dp"),
        P(None, "ctx", "dp"),
        P("dp"),
    )
    out_specs = (P("ctx", None, "dp"), P(None, "ctx", "dp"))
    return jax.shard_map(body, mesh=mesh, in_specs=in_specs, out_specs=out_specs, check_vma=False)
```

profile of v0, /device:TPU:1, one launch (start us, length us, event | category | flops | bytes accessed | tf_op | source)
XLA Modules:
  0.0 134.9 jit_solution(10038455365326142475)
XLA Ops:
  0.6 1.7 %copy.64 = bf16[256,2,128]{0,1,2:T(2,128)(2,1)} copy(bf16[256,2,128]{2,1,0:T(2,128)(2,1)} %param.7) | data formatting | bytes 262144 | tf_op args[2]
  2.4 14.3 %all-to-all-start.3 = ((bf16[256,2,128]{0,1,2:T(2,128)(2,1)}), bf16[256,2,128]{0,1,2:T(2,128)(2,1)S(1)}, u32[]{:S(2)}, u32[]{:S(2)}) async-start(bf16[256,2,128]{0,1,2:T(2,128)(2,1)} %copy.64), calls=%async_computation.3 | async-start | bytes 262144 | tf_op jit(solution)/shard_map/all_to_all | solution.py:116
  16.8 1.0 multiply_convert_fusion
  17.8 0.8 copy.58
  18.6 0.7 dynamic_slice.3
  19.3 7.4 %all-to-all-done.3 = bf16[256,2,128]{0,1,2:T(2,128)(2,1)S(1)} async-done(((bf16[256,2,128]{0,1,2:T(2,128)(2,1)}), bf16[256,2,128]{0,1,2:T(2,128)(2,1)S(1)}, u32[]{:S(2)}, u32[]{:S(2)}) %all-to-all-start.3) | async-done | bytes 131104 | tf_op jit(solution)/shard_map/all_to_all | solution.py:116
  26.8 4.0 %all-to-all-start = ((bf16[256,2,128]{0,1,2:T(2,128)(2,1)}), bf16[256,2,128]{0,1,2:T(2,128)(2,1)S(1)}, u32[]{:S(2)}, u32[]{:S(2)}) async-start(bf16[256,2,128]{0,1,2:T(2,128)(2,1)} %copy.58), calls=%async_computation | async-start | bytes 262144 | tf_op jit(solution)/shard_map/all_to_all | solution.py:115
  30.8 0.5 fusion.105
  31.8 8.9 %all-to-all-done = bf16[256,2,128]{0,1,2:T(2,128)(2,1)S(1)} async-done(((bf16[256,2,128]{0,1,2:T(2,128)(2,1)}), bf16[256,2,128]{0,1,2:T(2,128)(2,1)S(1)}, u32[]{:S(2)}, u32[]{:S(2)}) %all-to-all-start) | async-done | bytes 131104 | tf_op jit(solution)/shard_map/all_to_all | solution.py:115
  40.8 10.5 %all-to-all-start.1 = ((f32[32,8,128]{2,1,0:T(8,128)}), f32[32,8,128]{2,1,0:T(8,128)S(1)}, u32[]{:S(2)}, u32[]{:S(2)}) async-start(f32[32,8,128]{2,1,0:T(8,128)} %param.8), calls=%async_computation.1 | async-start | bytes 262144 | tf_op jit(solution)/shard_map/all_to_all | solution.py:121
  52.4 0.7 fusion.40
  53.1 0.7 fusion.41
  53.8 1.5 %fusion.2 = f32[64,65,16]{1,0,2:T(8,128)} fusion(f32[65,64,16]{0,1,2:T(8,128)S(1)} %fusion.40, f32[64,128,16]{1,0,2:T(8,128)S(1)} %fusion.105, f32[64,128,16]{1,0,2:T(8,128)S(1)} %fusion.112, f32[64,128]{1,0:T(8,128)S(1)} %get-tuple-element.20, f32[64,128]{1,0:T(8,128)S(1)} %get-tuple-element.21), kind=kOutput, calls=%fused_computation.5 | convolution fusion | flops 102812416 | bytes 1646592 | tf_op jit(solution)/shard_map/kac,ae->kec/dot_general | solution.py:61
  55.4 0.7 fusion.39
  56.1 1.5 %fusion.7 = f32[64,65,16]{1,0,2:T(8,128)} fusion(f32[65,64,16]{0,1,2:T(8,128)S(1)} %fusion.39, f32[64,128,16]{1,0,2:T(8,128)S(1)} %fusion.109, f32[64,128,16]{1,0,2:T(8,128)S(1)} %fusion.116, f32[64,128]{1,0:T(8,128)S(1)} %get-tuple-element.20, f32[64,128]{1,0:T(8,128)S(1)} %get-tuple-element.21), kind=kOutput, calls=%fused_computation.15 | convolution fusion | flops 102820736 | bytes 1646592 | tf_op jit(solution)/shard_map/kac,ae->kec/dot_general | solution.py:58
  57.6 1.6 %fusion.3 = f32[64,65,16]{1,0,2:T(8,128)} fusion(f32[65,64,16]{0,1,2:T(8,128)S(1)} %fusion.41, f32[64,128,16]{1,0,2:T(8,128)S(1)} %fusion.105, f32[64,128,16]{1,0,2:T(8,128)S(1)} %fusion.112, f32[64,128]{1,0:T(8,128)S(1)} %get-tuple-element.20, f32[64,128]{1,0:T(8,128)S(1)} %get-tuple-element.21), kind=kOutput, calls=%fused_computation.7 | convolution fusion | flops 102820736 | bytes 1646592 | tf_op jit(solution)/shard_map/kac,ae->kec/dot_general | solution.py:58
  59.2 1.5 %fusion.38 = f32[65,64,16]{0,1,2:T(8,128)} fusion(f32[64,128,16]{1,0,2:T(8,128)S(1)} %fusion.109, f32[64,128,16]{1,0,2:T(8,128)S(1)} %fusion.116, f32[64,128]{1,0:T(8,128)S(1)} %get-tuple-element.20, f32[64,128]{1,0:T(8,128)S(1)} %get-tuple-element.21), kind=kOutput, calls=%fused_computation.64 | convolution fusion | flops 102754176 | bytes 1380352 | tf_op jit(solution)/shard_map/kac,ae->kec/dot_general | solution.py:61
  61.7 0.5 fusion.48
  62.3 0.5 fusion.49
  62.8 0.5 fusion.8
  63.3 0.5 fusion.9
  63.9 1.0 add_multiply_fusion
  64.9 0.7 fusion.69
  65.6 0.7 fusion.71
  66.3 0.7 fusion.4
  67.1 0.9 fusion.5
  69.2 2.8 %copy.61 = bf16[4096,2,8]{2,1,0:T(2,128)(2,1)S(1)} copy(bf16[4096,2,8]{0,2,1:T(8,128)(2,1)S(1)} %fusion.29) | data formatting | bytes 262144 | tf_op jit(solution)/shard_map/convert_element_type | solution.py:137
  72.0 2.8 %reshape.120 = bf16[16,2,2048]{2,1,0:T(2,128)(2,1)} reshape(bf16[4096,2,8]{2,1,0:T(2,128)(2,1)S(1)} %copy.61) | data formatting | bytes 262144
  74.8 5.4 %all-to-all-start.2 = ((bf16[16,2,2048]{2,1,0:T(2,128)(2,1)}), bf16[16,2,2048]{2,1,0:T(2,128)(2,1)S(1)}, u32[]{:S(2)}, u32[]{:S(2)}) async-start(bf16[16,2,2048]{2,1,0:T(2,128)(2,1)} %reshape.120), calls=%async_computation.2 | async-start | bytes 262144 | tf_op jit(solution)/shard_map/all_to_all | solution.py:138
  80.2 0.7 fusion.63
  80.9 0.7 fusion.65
  81.7 0.7 fusion
  82.4 0.7 fusion.1
  83.1 0.5 fusion.17
  83.6 0.5 convolution_add_fusion.4
  84.2 2.5 %copy.67 = f32[1,8,4096]{1,0,2:T(1,128)S(1)} copy(f32[1,8,4096]{2,1,0:T(8,128)S(1)} %multiply_bitcast_fusion) | data formatting | bytes 262144 | tf_op jit(solution)/shard_map/broadcast_in_dim | solution.py:135
  86.7 0.5 broadcast.239
  87.2 19.3 %reduce = f32[4096,8]{1,0:T(8,128)} reduce(f32[4096,1,8]{2,1,0:T(1,128)S(1)} %bitcast.171, f32[]{:T(128)} %broadcast.239), dimensions={1}, to_apply=%bitcast.154.reduce_sub_computation | reduce | bytes 262148
  106.5 3.3 %reshape.122 = f32[32,1,1024]{2,1,0:T(1,128)} reshape(f32[4096,8]{1,0:T(8,128)} %reduce) | data formatting | bytes 262144
  109.9 8.9 %all-to-all-start.4 = ((f32[32,1,1024]{2,1,0:T(1,128)}), f32[32,1,1024]{2,1,0:T(1,128)S(1)}, u32[]{:S(2)}, u32[]{:S(2)}) async-start(f32[32,1,1024]{2,1,0:T(1,128)} %reshape.122), calls=%async_computation.4 | async-start | bytes 262144 | tf_op jit(solution)/shard_map/all_to_all | solution.py:136
  118.8 2.5 %reshape.121 = bf16[4096,2,8]{2,1,0:T(2,128)(2,1)S(1)} reshape(bf16[16,2,2048]{2,1,0:T(2,128)(2,1)S(1)} %all-to-all-done.2) | data formatting | bytes 262144
  121.2 1.2 copy.72
  122.5 0.8 copy.69
  123.3 4.7 %all-to-all-done.4 = f32[32,1,1024]{2,1,0:T(1,128)S(1)} async-done(((f32[32,1,1024]{2,1,0:T(1,128)}), f32[32,1,1024]{2,1,0:T(1,128)S(1)}, u32[]{:S(2)}, u32[]{:S(2)}) %all-to-all-start.4) | async-done | bytes 131104 | tf_op jit(solution)/shard_map/all_to_all | solution.py:136
  127.9 0.9 reduce.1
  128.8 3.5 %reshape.123 = f32[4096,1,8]{2,1,0:T(1,128)S(1)} reshape(f32[32,1024]{1,0:T(8,128)S(1)} %reduce.1) | data formatting | bytes 262144
  132.3 1.9 %copy.68 = f32[1,8,4096]{2,0,1:T(1,128)S(1)} copy(f32[1,8,4096]{1,0,2:T(1,128)S(1)} %bitcast.173) | data formatting | bytes 262144 | tf_op jit(solution)/shard_map/all_to_all | solution.py:136
  134.2 0.7 copy.70
  (31 shorter events, 4.1 us)
Async XLA Ops:
  2.4 24.4 %all-to-all-start.3 = ((bf16[256,2,128]{0,1,2:T(2,128)(2,1)}), bf16[256,2,128]{0,1,2:T(2,128)(2,1)S(1)}, u32[]{:S(2)}, u32[]{:S(2)}) async-start(bf16[256,2,128]{0,1,2:T(2,128)(2,1)} %copy.64), calls=%async_computation.3 | async-start | bytes 262144 | tf_op jit(solution)/shard_map/all_to_all | solution.py:116
  26.8 14.0 %all-to-all-start = ((bf16[256,2,128]{0,1,2:T(2,128)(2,1)}), bf16[256,2,128]{0,1,2:T(2,128)(2,1)S(1)}, u32[]{:S(2)}, u32[]{:S(2)}) async-start(bf16[256,2,128]{0,1,2:T(2,128)(2,1)} %copy.58), calls=%async_computation | async-start | bytes 262144 | tf_op jit(solution)/shard_map/all_to_all | solution.py:115
  40.8 19.9 %all-to-all-start.1 = ((f32[32,8,128]{2,1,0:T(8,128)}), f32[32,8,128]{2,1,0:T(8,128)S(1)}, u32[]{:S(2)}, u32[]{:S(2)}) async-start(f32[32,8,128]{2,1,0:T(8,128)} %param.8), calls=%async_computation.1 | async-start | bytes 262144 | tf_op jit(solution)/shard_map/all_to_all | solution.py:121
  61.2 2.6 %copy-start = (f32[65,64,16]{0,1,2:T(8,128)S(1)}, f32[65,64,16]{0,1,2:T(8,128)}, u32[]{:S(2)}) copy-start(f32[65,64,16]{0,1,2:T(8,128)} %fusion.38) | copy-start | bytes 798724
  61.2 2.6 %copy-start.1 = (f32[64,65,16]{1,0,2:T(8,128)S(1)}, f32[64,65,16]{1,0,2:T(8,128)}, u32[]{:S(2)}) copy-start(f32[64,65,16]{1,0,2:T(8,128)} %fusion.2) | copy-start | bytes 798724
  61.2 2.6 %copy-start.2 = (f32[64,65,16]{1,0,2:T(8,128)S(1)}, f32[64,65,16]{1,0,2:T(8,128)}, u32[]{:S(2)}) copy-start(f32[64,65,16]{1,0,2:T(8,128)} %fusion.7) | copy-start | bytes 798724
  61.2 2.6 %copy-start.3 = (f32[64,65,16]{1,0,2:T(8,128)S(1)}, f32[64,65,16]{1,0,2:T(8,128)}, u32[]{:S(2)}) copy-start(f32[64,65,16]{1,0,2:T(8,128)} %fusion.3) | copy-start | bytes 798724
  74.8 35.0 %all-to-all-start.2 = ((bf16[16,2,2048]{2,1,0:T(2,128)(2,1)}), bf16[16,2,2048]{2,1,0:T(2,128)(2,1)S(1)}, u32[]{:S(2)}, u32[]{:S(2)}) async-start(bf16[16,2,2048]{2,1,0:T(2,128)(2,1)} %reshape.120), calls=%async_computation.2 | async-start | bytes 262144 | tf_op jit(solution)/shard_map/all_to_all | solution.py:138
  109.9 18.1 %all-to-all-start.4 = ((f32[32,1,1024]{2,1,0:T(1,128)}), f32[32,1,1024]{2,1,0:T(1,128)S(1)}, u32[]{:S(2)}, u32[]{:S(2)}) async-start(f32[32,1,1024]{2,1,0:T(1,128)} %reshape.122), calls=%async_computation.4 | async-start | bytes 262144 | tf_op jit(solution)/shard_map/all_to_all | solution.py:136
where the time goes:
time: 136 us; the launch traced here: 135 us
  starting transfers between devices  43 us (32%)
  local copies, waits for them, and re-layouts  26.1 us (19%)
  matrix products  22.3 us (16%)
  other arithmetic  21.5 us (16%)
  waiting for transfers between devices  21.1 us (16%)
    unnamed x1, other arithmetic  19.3 us
    unnamed x16, local copies, waits for them, and re-layouts  15.9 us
    all_to_all x1, starting transfers between devices, body(): lax.all_to_all(conv_input, 'ctx', split_axis=2, concat_axis=0, tiled=True)  14.3 us
    all_to_all x1, starting transfers between devices, body(): lax.all_to_all(filters, 'dp', split_axis=0, concat_axis=2, tiled=True)  10.5 us
    all_to_all x1, waiting for transfers between devices, body(): lax.all_to_all(gate_grad, 'ctx', split_axis=2, concat_axis=0, tiled=True)  8.94 us
    all_to_all x1, starting transfers between devices, body(): lax.all_to_all(lag_grad, 'dp', split_axis=2, concat_axis=0, tiled=True)  8.92 us
    all_to_all x1, waiting for transfers between devices, body(): lax.all_to_all(conv_input, 'ctx', split_axis=2, concat_axis=0, tiled=True)  7.44 us
    all_to_all x1, starting transfers between devices, body(): lax.all_to_all(spread, 'ctx', split_axis=0, concat_axis=2, tiled=True)  5.39 us
  transfers between devices with their start and end apart: 5, of which 3 were waited for; matrix products, arithmetic and copies ran while one was open for 35% of the time, Pallas kernels for 0%

commit v1 on v0

v1 whole, which is shorter than its diff:
```python
import functools

import jax
import jax.numpy as jnp
from jax import lax
from jax.experimental import pallas as pl
from jax.experimental.pallas import tpu as pltpu
from jax.sharding import PartitionSpec as P

MESH = pl.DeviceIdType.MESH
F32 = jnp.float32
BF16 = jnp.bfloat16

SPAN = 512
HOP = 16
LANES = 128
OWN = 8
SEQ = 2


def lane_index(shape):
    return lax.broadcasted_iota(jnp.int32, shape, len(shape) - 1)


def row_index(shape):
    return lax.broadcasted_iota(jnp.int32, shape, len(shape) - 2)


def swap_groups(blocks):
    blocks = list(blocks)
    lane = lane_index((HOP, LANES)) // HOP
    for bit in (1, 2, 4):
        upper = (lane & bit) != 0
        for r in range(8):
            if r & bit:
                continue
            low, high = blocks[r], blocks[r | bit]
            blocks[r] = jnp.where(upper, pltpu.roll(high, HOP * bit, 1), low)
            blocks[r | bit] = jnp.where(upper, high, pltpu.roll(low, LANES - HOP * bit, 1))
    return blocks


def spread_rows(wide_ref, send_ref):
    halves = []
    for s in range(SEQ):
        part = wide_ref[pl.ds(s, 256, stride=2), :]
        halves.append(part.T.reshape(16, OWN, 256))
    send_ref[...] = jnp.concatenate(halves, axis=1).astype(BF16)


def build_toeplitz(hwide_ref, toep_ref, c):
    tiles = [hwide_ref[pl.ds(OWN * h + c, 8, stride=32), :] for h in range(4)]
    before = jnp.where(row_index((8, LANES)) == 0, 0.0, pltpu.roll(tiles[3], 1, 0))
    tiles = [before] + tiles
    keep = lane_index((HOP, LANES)) >= row_index((HOP, LANES))
    for q in range(8):
        turned = [
            pltpu.roll(jnp.broadcast_to(tile[q : q + 1, :], (HOP, LANES)), 0, 1, stride=1, stride_axis=0)
            for tile in tiles
        ]
        rows = [jnp.where(keep, turned[h + 1], turned[h]) for h in range(4)]
        toep_ref[c, q * HOP : (q + 1) * HOP, :] = jnp.concatenate(rows, axis=1).astype(BF16)


def own_rows(wide_ref, c):
    seqs = []
    for s in range(SEQ):
        seqs.append(
            jnp.concatenate(
                [
                    wide_ref[v, pl.ds(h * 16 + s * OWN + c, 8, stride=32), :]
                    for h in range(2)
                    for v in range(2)
                ],
                axis=1,
            )
        )
    return jnp.concatenate(seqs, axis=0)


def build_windows(gwide_ref, win_ref, c):
    here = own_rows(gwide_ref, c)
    after = pltpu.roll(here, 15, 0)
    after = jnp.where(row_index((16, SPAN)) % 8 == 7, 0.0, after)
    both = jnp.concatenate([here, after], axis=1)
    for r in range(8):
        turned = both if r == 0 else pltpu.roll(both, 2 * SPAN - HOP * r, 1)
        for jt in range(4):
            j = 8 * jt + r
            win_ref[c, j * 16 : (j + 1) * 16, :] = turned[:, LANES * jt : LANES * jt + SPAN].astype(BF16)


def back_rows(toep_ref, win_ref, yall_ref, c):
    out = lax.dot_general(
        toep_ref[c], win_ref[c], (((1,), (1,)), ((), ())), preferred_element_type=F32
    )
    group = lane_index((HOP, LANES)) % 8
    cols = []
    for n in range(4):
        tile = out[:, n * LANES : (n + 1) * LANES]
        total = tile[0:HOP]
        for q in range(1, 8):
            turned = pltpu.roll(tile[q * HOP : (q + 1) * HOP], LANES - q, 1)
            total = total + jnp.where(group < 8 - q, turned, 0.0)
        cols.append(total)
    yall_ref[pl.ds(pl.multiple_of(c * HOP, HOP), HOP), :] = jnp.concatenate(cols, axis=1)


def finish_back(yall_ref, gwide_ref, gain_ref, first_gain, ywide_ref):
    cols = []
    for n in range(4):
        turned = yall_ref[:, n * LANES : (n + 1) * LANES].T
        cols.append(swap_groups([turned[HOP * r : HOP * (r + 1)] for r in range(8)]))
    for c in range(OWN):
        rows = jnp.concatenate([cols[n][c] for n in range(4)], axis=1)
        rows = rows + gain_ref[first_gain + c] * own_rows(gwide_ref, c)
        for s in range(SEQ):
            for h in range(2):
                for v in range(2):
                    n = 2 * h + v
                    ywide_ref[v, pl.ds(h * 16 + s * OWN + c, 8, stride=32), :] = rows[
                        8 * s : 8 * s + 8, n * LANES : (n + 1) * LANES
                    ]


def turn_inputs(xwide_ref, xall_ref):
    rows = [own_rows(xwide_ref, c) for c in range(OWN)]
    for n in range(4):
        blocks = swap_groups([row[:, n * LANES : (n + 1) * LANES] for row in rows])
        xall_ref[:, n * LANES : (n + 1) * LANES] = jnp.concatenate(blocks, axis=0).T


def filter_rows(xall_ref, xs_ref, win_ref, dwide_ref, c):
    keep = (lane_index((8, LANES)) % 8) >= row_index((8, LANES))
    for pair in range(8):
        rows = []
        for a in (2 * pair, 2 * pair + 1):
            line = xall_ref[pl.ds(c * HOP + a, 1), :]
            tiles = []
            for n in range(4):
                wide = jnp.broadcast_to(line[:, n * LANES : (n + 1) * LANES], (8, LANES))
                turned = pltpu.roll(wide, 0, 1, stride=1, stride_axis=0)
                tiles.append(jnp.where(keep, turned, 0.0))
            rows.append(jnp.concatenate(tiles, axis=1))
        xs_ref[pair * 16 : (pair + 1) * 16, :] = jnp.concatenate(rows, axis=0).astype(BF16)
    out = jnp.dot(xs_ref[...], win_ref[c], preferred_element_type=F32)
    lane = lane_index((8, LANES))
    sums = [out[0:8, n * LANES : (n + 1) * LANES] for n in range(4)]
    wrapped = jnp.zeros((8, LANES), F32)
    for a in range(1, HOP):
        turned = [
            pltpu.roll(out[8 * a : 8 * a + 8, n * LANES : (n + 1) * LANES], LANES - a, 1) for n in range(4)
        ]
        inside = lane < LANES - a
        for n in range(3):
            sums[n] = sums[n] + jnp.where(inside, turned[n], turned[n + 1])
        sums[3] = sums[3] + jnp.where(inside, turned[3], 0.0)
        wrapped = wrapped + jnp.where(inside, 0.0, turned[0])
    wrapped = jnp.where(row_index((8, LANES)) == 7, 0.0, pltpu.roll(wrapped, 7, 0))
    sums[3] = sums[3] + wrapped
    for h in range(4):
        dwide_ref[pl.ds(OWN * h + c, 8, stride=32), :] = sums[h] * (1.0 / SEQ)


def widen(ref, wide_ref):
    for v in range(2):
        wide_ref[v] = ref[:, :, v * LANES : (v + 1) * LANES].astype(F32).reshape(256, LANES)


def kernel(
    n_ctx, n_dp,
    up_ref, gate_ref, in_ref, filt_ref, gain_ref,
    out_ref, grad_ref,
    wide, gsend, xsend, grecv, xrecv, hrecv, gwide, xwide, toep, win, yall, ysend, yrecv, xall, xs, dsend,
    h_send_sem, h_recv_sem, g_send_sem, g_recv_sem, x_send_sem, x_recv_sem,
    y_send_sem, y_recv_sem, d_send_sem, d_recv_sem,
):
    me_ctx = lax.axis_index("ctx")
    me_dp = lax.axis_index("dp")

    def over_ctx(step):
        peer = lax.rem(me_ctx + step, n_ctx)
        return peer, {"ctx": peer, "dp": me_dp}

    def over_dp(step):
        peer = lax.rem(me_dp + step, n_dp)
        return peer, {"ctx": me_ctx, "dp": peer}

    barrier = pltpu.get_barrier_semaphore()

    @pl.loop(1, n_ctx)
    def _(step):
        pl.semaphore_signal(barrier, inc=1, device_id=over_ctx(step)[1], device_id_type=MESH)

    @pl.loop(1, n_dp)
    def _(step):
        pl.semaphore_signal(barrier, inc=1, device_id=over_dp(step)[1], device_id_type=MESH)

    def scatter(count, over, me, src, dst, send_sem, recv_sem):
        own = pltpu.make_async_copy(src.at[me], dst.at[me], recv_sem)
        own.start()

        @pl.loop(1, count)
        def _(step):
            peer, where = over(step)
            pltpu.make_async_remote_copy(
                src_ref=src.at[peer], dst_ref=dst.at[me], send_sem=send_sem, recv_sem=recv_sem,
                device_id=where, device_id_type=MESH,
            ).start()

    def arrive(dst, sem):
        pltpu.make_async_copy(dst, dst, sem).wait()

    def sent(count, src, sem):
        part = src.at[pl.ds(0, count - 1)]
        pltpu.make_async_copy(part, part, sem).wait()

    wide[...] = (up_ref[...].astype(F32) * gate_ref[...].astype(F32)).astype(BF16).astype(F32)
    spread_rows(wide, gsend)

    pl.semaphore_wait(barrier, n_ctx + n_dp - 2)
    scatter(n_dp, over_dp, me_dp, filt_ref, hrecv, h_send_sem, h_recv_sem)
    scatter(n_ctx, over_ctx, me_ctx, gsend, grecv, g_send_sem, g_recv_sem)
    wide[...] = in_ref[...].astype(F32)
    spread_rows(wide, xsend)
    scatter(n_ctx, over_ctx, me_ctx, xsend, xrecv, x_send_sem, x_recv_sem)

    arrive(hrecv, h_recv_sem)
    hwide = hrecv.reshape(n_dp * OWN, LANES)

    @pl.loop(0, OWN)
    def _(c):
        build_toeplitz(hwide, toep, c)

    arrive(grecv, g_recv_sem)
    widen(grecv, gwide)

    @pl.loop(0, OWN)
    def _(c):
        build_windows(gwide, win, c)
        back_rows(toep, win, yall, c)

    finish_back(yall, gwide, gain_ref, me_ctx * OWN, xwide)
    for v in range(2):
        ysend[:, :, v * LANES : (v + 1) * LANES] = xwide[v].reshape(16, 16, LANES).astype(BF16)
    scatter(n_ctx, over_ctx, me_ctx, ysend, yrecv, y_send_sem, y_recv_sem)

    arrive(xrecv, x_recv_sem)
    widen(xrecv, xwide)
    turn_inputs(xwide, xall)
    dwide = dsend.reshape(n_dp * OWN, LANES)

    @pl.loop(0, OWN)
    def _(c):
        filter_rows(xall, xs, win, dwide, c)

    scatter(n_dp, over_dp, me_dp, dsend, grad_ref, d_send_sem, d_recv_sem)

    arrive(yrecv, y_recv_sem)
    back = yrecv[...].astype(F32)
    for s in range(SEQ):
        wide[pl.ds(s, 256, stride=2), :] = back[:, s * OWN : (s + 1) * OWN, :].reshape(16 * OWN, 256).T
    out_ref[...] = wide[...].astype(BF16)

    arrive(grad_ref, d_recv_sem)
    sent(n_dp, filt_ref, h_send_sem)
    sent(n_ctx, gsend, g_send_sem)
    sent(n_ctx, xsend, x_send_sem)
    sent(n_ctx, ysend, y_send_sem)
    sent(n_dp, dsend, d_send_sem)


def body(upstream, gate_value, conv_input, filters, skip_gain):
    n_ctx = lax.axis_size("ctx")
    n_dp = lax.axis_size("dp")
    rows = upstream.shape[0] * upstream.shape[1]
    width = upstream.shape[2]
    vmem = pl.BlockSpec(memory_space=pltpu.VMEM)
    block = (16, 16, 256)
    back, grads = pl.pallas_call(
        functools.partial(kernel, n_ctx, n_dp),
        out_shape=(
            jax.ShapeDtypeStruct((rows, width), BF16),
            jax.ShapeDtypeStruct(filters.shape, F32),
        ),
        in_specs=[vmem, vmem, vmem, pl.BlockSpec(memory_space=pltpu.VMEM), pl.BlockSpec(memory_space=pltpu.SMEM)],
        out_specs=(vmem, vmem),
        scratch_shapes=[
            pltpu.VMEM((rows, width), F32),
            pltpu.VMEM(block, BF16),
            pltpu.VMEM(block, BF16),
            pltpu.VMEM(block, BF16),
            pltpu.VMEM(block, BF16),
            pltpu.VMEM(filters.shape, F32),
            pltpu.VMEM((2, 256, LANES), F32),
            pltpu.VMEM((2, 256, LANES), F32),
            pltpu.VMEM((OWN, 8 * HOP, SPAN), BF16),
            pltpu.VMEM((OWN, SPAN, SPAN), BF16),
            pltpu.VMEM((OWN * HOP, SPAN), F32),
            pltpu.VMEM(block, BF16),
            pltpu.VMEM(block, BF16),
            pltpu.VMEM((OWN * HOP, SPAN), F32),
            pltpu.VMEM((8 * HOP, SPAN), BF16),
            pltpu.VMEM(filters.shape, F32),
        ]
        + [pltpu.SemaphoreType.DMA] * 10,
        compiler_params=pltpu.CompilerParams(
            collective_id=0, has_side_effects=True, vmem_limit_bytes=32 * 1024 * 1024
        ),
    )(
        upstream.reshape(rows, width),
        gate_value.reshape(rows, width),
        conv_input.reshape(rows, width),
        filters,
        skip_gain,
    )
    return back.reshape(upstream.shape), grads


def solution(mesh):
    in_specs = (
        P("ctx", None, "dp"),
        P("ctx", None, "dp"),
        P("ctx", None, "dp"),
        P(None, "ctx", "dp"),
        P("dp"),
    )
    out_specs = (P("ctx", None, "dp"), P(None, "ctx", "dp"))
    return jax.shard_map(body, mesh=mesh, in_specs=in_specs, out_specs=out_specs, check_vma=False)
```

time: 136 us -> 48.5 us (0.36)
  starting transfers between devices: 43 us -> 0 us
  Pallas kernels: 0 us -> 42.1 us
  matrix products: 22.3 us -> 0 us
  other arithmetic: 21.5 us -> 0 us
  waiting for transfers between devices: 21.1 us -> 0 us
  local copies, waits for them, and re-layouts: 26.1 us -> 5.58 us
    all_to_all x5 -> x0, starting transfers between devices: 43 us -> none  [the longest x1 14.3 us: body(): lax.all_to_all(conv_input, 'ctx', split_axis=2, concat_axis=0, tiled=True)]
    pallas_call x0 -> x1, Pallas kernels: none -> 42.1 us  [body(): pl.pallas_call(functools.partial(kernel, n_ctx, n_dp), out_shape=(jax.Sha...]
    dot_general x30 -> x0, matrix products: 22.3 us -> none  [the longest x3 3.61 us: spectrum(): jnp.einsum('kac,ae->kec', turned_imag, sin_inner, precision=precise)]
    all_to_all x5 -> x0, waiting for transfers between devices: 21.1 us -> none  [the longest x1 8.94 us: body(): lax.all_to_all(gate_grad, 'ctx', split_axis=2, concat_axis=0, tiled=True)]
    unnamed x1 -> x0, other arithmetic: 19.3 us -> none
    unnamed x16 -> x12, local copies, waits for them, and re-layouts: 15.9 us -> 5.58 us
    convert_element_type x2 -> x0, local copies, waits for them, and re-layouts: 3.57 us -> none  [the longest x1 2.78 us: body(): output_cols.astype(jnp.bfloat16).reshape(seqlen, seq_count, own_width)]
    all_to_all x6 -> x0, local copies, waits for them, and re-layouts: 3.19 us -> none  [the longest x1 1.87 us: body(): lax.all_to_all(lag_grad, 'dp', split_axis=2, concat_axis=0, tiled=True)]
  transfers between devices with their start and end apart: 5 -> 0, of which waited for: 3 -> 0; matrix products, arithmetic and copies ran while one was open for 35% -> 0% of each run, Pallas kernels for 0% -> 0%
where the time goes in v1:
time: 48.5 us; the launch traced here: 48.3 us
  Pallas kernels  42.1 us (87%)
  local copies, waits for them, and re-layouts  5.58 us (12%)
  between operations  0.65 us (1%)
    pallas_call x1, Pallas kernels, body(): pl.pallas_call(functools.partial(kernel, n_ctx, n_dp), out_shape=(jax.Sha...  42.1 us
    unnamed x12, local copies, waits for them, and re-layouts  5.58 us

profile of v1, /device:TPU:1, one launch (start us, length us, event | category | flops | bytes accessed | tf_op | source)
XLA Modules:
  0.0 48.3 jit_solution(15155809565198544881)
XLA Ops:
  0.6 0.0 copy-start.4
  0.6 0.6 %copy-done.4 = f32[128]{0:T(128)S(1)} copy-done((f32[128]{0:T(128)S(1)}, f32[128]{0:T(128)}, u32[]{:S(2)}) %copy-start.4) | copy-done | bytes 536
  1.3 0.0 copy-start
  1.3 0.9 %copy-done = bf16[256,2,128]{2,1,0:T(2,128)(2,1)S(1)} copy-done((bf16[256,2,128]{2,1,0:T(2,128)(2,1)S(1)}, bf16[256,2,128]{2,1,0:T(2,128)(2,1)}, u32[]{:S(2)}) %copy-start) | copy-done | bytes 131096
  2.2 0.0 copy-start.1
  2.2 0.9 %copy-done.1 = bf16[256,2,128]{2,1,0:T(2,128)(2,1)S(1)} copy-done((bf16[256,2,128]{2,1,0:T(2,128)(2,1)S(1)}, bf16[256,2,128]{2,1,0:T(2,128)(2,1)}, u32[]{:S(2)}) %copy-start.1) | copy-done | bytes 131096
  3.1 0.0 copy-start.2
  3.1 0.9 %copy-done.2 = bf16[256,2,128]{2,1,0:T(2,128)(2,1)S(1)} copy-done((bf16[256,2,128]{2,1,0:T(2,128)(2,1)S(1)}, bf16[256,2,128]{2,1,0:T(2,128)(2,1)}, u32[]{:S(2)}) %copy-start.2) | copy-done | bytes 131096
  4.0 0.0 copy-start.3
  4.0 0.9 %copy-done.3 = f32[32,8,128]{2,1,0:T(8,128)S(1)} copy-done((f32[32,8,128]{2,1,0:T(8,128)S(1)}, f32[32,8,128]{2,1,0:T(8,128)}, u32[]{:S(2)}) %copy-start.3) | copy-done | bytes 131096
  4.9 42.1 %shard_map.68 = (bf16[512,128]{1,0:T(8,128)(2,1)S(1)}, f32[32,8,128]{2,1,0:T(8,128)S(1)}) custom-call(bf16[512,128]{1,0:T(8,128)(2,1)S(1)} %bitcast.4, bf16[512,128]{1,0:T(8,128)(2,1)S(1)} %bitcast.5, bf16[512,128]{1,0:T(8,128)(2,1)S(1)} %bitcast.6, f32[32,8,128]{2,1,0:T(8,128)S(1)} %copy-done.3, f32[128]{0:T(128)S(1)} %copy-done.4), custom_call_target="tpu_custom_call" | custom-call | tf_op jit(solution)/shard_map/pallas_call | solution.py:280
  47.0 0.7 %copy.9 = bf16[256,2,128]{2,1,0:T(2,128)(2,1)} copy(bf16[256,2,128]{2,1,0:T(2,128)(2,1)S(1)} %bitcast.7) | data formatting | bytes 262144
  47.7 0.7 %copy.10 = f32[32,8,128]{2,1,0:T(8,128)} copy(f32[32,8,128]{2,1,0:T(8,128)S(1)} %get-tuple-element.9) | data formatting | bytes 262144
Async XLA Ops:
  0.6 0.7 %copy-start.4 = (f32[128]{0:T(128)S(1)}, f32[128]{0:T(128)}, u32[]{:S(2)}) copy-start(f32[128]{0:T(128)} %gain_ref.1) | copy-start | bytes 1540
  1.3 0.9 %copy-start = (bf16[256,2,128]{2,1,0:T(2,128)(2,1)S(1)}, bf16[256,2,128]{2,1,0:T(2,128)(2,1)}, u32[]{:S(2)}) copy-start(bf16[256,2,128]{2,1,0:T(2,128)(2,1)} %param.5) | copy-start | bytes 393220
  2.2 0.9 %copy-start.1 = (bf16[256,2,128]{2,1,0:T(2,128)(2,1)S(1)}, bf16[256,2,128]{2,1,0:T(2,128)(2,1)}, u32[]{:S(2)}) copy-start(bf16[256,2,128]{2,1,0:T(2,128)(2,1)} %param.6) | copy-start | bytes 393220
  3.1 0.9 %copy-start.2 = (bf16[256,2,128]{2,1,0:T(2,128)(2,1)S(1)}, bf16[256,2,128]{2,1,0:T(2,128)(2,1)}, u32[]{:S(2)}) copy-start(bf16[256,2,128]{2,1,0:T(2,128)(2,1)} %param.7) | copy-start | bytes 393220
  4.0 0.9 %copy-start.3 = (f32[32,8,128]{2,1,0:T(8,128)S(1)}, f32[32,8,128]{2,1,0:T(8,128)}, u32[]{:S(2)}) copy-start(f32[32,8,128]{2,1,0:T(8,128)} %filt_ref.1) | copy-start | bytes 393220

commit v2 on v1

--- a/solution.py
+++ b/solution.py
@@ -170,37 +170,53 @@
 def kernel(
     n_ctx, n_dp,
     up_ref, gate_ref, in_ref, filt_ref, gain_ref,
-    out_ref, grad_ref,
-    wide, gsend, xsend, grecv, xrecv, hrecv, gwide, xwide, toep, win, yall, ysend, yrecv, xall, xs, dsend,
+    yrecv, drecv,
+    up, gate, raw, filt, gain, wide, gsend, xsend, hsend, grecv, xrecv, hrecv, gwide, xwide, hwide, toep, win,
+    yall, ysend, xall, xs, dwide, dsend,
+    load_sem,
     h_send_sem, h_recv_sem, g_send_sem, g_recv_sem, x_send_sem, x_recv_sem,
     y_send_sem, y_recv_sem, d_send_sem, d_recv_sem,
 ):
     me_ctx = lax.axis_index("ctx")
     me_dp = lax.axis_index("dp")
-
-    def over_ctx(step):
-        peer = lax.rem(me_ctx + step, n_ctx)
+    half = n_ctx // 2
+    me_hi = me_ctx // half
+    me_lo = lax.rem(me_ctx, half)
+
+    def far_ctx(step):
+        peer = (1 - me_hi) * half + lax.rem(me_lo + step, half)
+        return peer, {"ctx": peer, "dp": me_dp}
+
+    def near_ctx(step):
+        peer = me_hi * half + lax.rem(me_lo + step, half)
         return peer, {"ctx": peer, "dp": me_dp}
 
     def over_dp(step):
         peer = lax.rem(me_dp + step, n_dp)
         return peer, {"ctx": me_ctx, "dp": peer}
 
+    loads = [
+        pltpu.make_async_copy(src, dst, load_sem.at[n])
+        for n, (src, dst) in enumerate(
+            ((up_ref, up), (gate_ref, gate), (in_ref, raw), (filt_ref, filt), (gain_ref, gain))
+        )
+    ]
+    for load in loads:
+        load.start()
+
     barrier = pltpu.get_barrier_semaphore()
 
-    @pl.loop(1, n_ctx)
-    def _(step):
-        pl.semaphore_signal(barrier, inc=1, device_id=over_ctx(step)[1], device_id_type=MESH)
-
-    @pl.loop(1, n_dp)
-    def _(step):
-        pl.semaphore_signal(barrier, inc=1, device_id=over_dp(step)[1], device_id_type=MESH)
-
-    def scatter(count, over, me, src, dst, send_sem, recv_sem):
-        own = pltpu.make_async_copy(src.at[me], dst.at[me], recv_sem)
-        own.start()
-
-        @pl.loop(1, count)
+    def greet(first, last, over):
+        @pl.loop(first, last)
+        def _(step):
+            pl.semaphore_signal(barrier, inc=1, device_id=over(step)[1], device_id_type=MESH)
+
+    greet(0, half, far_ctx)
+    greet(1, n_dp, over_dp)
+    greet(1, half, near_ctx)
+
+    def scatter(first, last, over, me, src, dst, send_sem, recv_sem):
+        @pl.loop(first, last)
         def _(step):
             peer, where = over(step)
             pltpu.make_async_remote_copy(
@@ -208,6 +224,9 @@
                 device_id=where, device_id_type=MESH,
             ).start()
 
+    def keep_own(me, src, dst, recv_sem):
+        pltpu.make_async_copy(src.at[me], dst.at[me], recv_sem).start()
+
     def arrive(dst, sem):
         pltpu.make_async_copy(dst, dst, sem).wait()
 
@@ -215,59 +234,85 @@
         part = src.at[pl.ds(0, count - 1)]
         pltpu.make_async_copy(part, part, sem).wait()
 
-    wide[...] = (up_ref[...].astype(F32) * gate_ref[...].astype(F32)).astype(BF16).astype(F32)
+    loads[0].wait()
+    loads[1].wait()
+    wide[...] = (up[...].astype(F32) * gate[...].astype(F32)).astype(BF16).astype(F32)
     spread_rows(wide, gsend)
+    loads[3].wait()
+    hsend[...] = filt[...].astype(BF16)
+    loads[2].wait()
+    wide[...] = raw[...].astype(F32)
+    spread_rows(wide, xsend)
 
     pl.semaphore_wait(barrier, n_ctx + n_dp - 2)
-    scatter(n_dp, over_dp, me_dp, filt_ref, hrecv, h_send_sem, h_recv_sem)
-    scatter(n_ctx, over_ctx, me_ctx, gsend, grecv, g_send_sem, g_recv_sem)
-    wide[...] = in_ref[...].astype(F32)
-    spread_rows(wide, xsend)
-    scatter(n_ctx, over_ctx, me_ctx, xsend, xrecv, x_send_sem, x_recv_sem)
+    scatter(0, half, far_ctx, me_ctx, gsend, grecv, g_send_sem, g_recv_sem)
+    scatter(1, n_dp, over_dp, me_dp, hsend, hrecv, h_send_sem, h_recv_sem)
+    scatter(1, half, near_ctx, me_ctx, gsend, grecv, g_send_sem, g_recv_sem)
+    scatter(0, half, far_ctx, me_ctx, xsend, xrecv, x_send_sem, x_recv_sem)
+    scatter(1, half, near_ctx, me_ctx, xsend, xrecv, x_send_sem, x_recv_sem)
+    keep_own(me_dp, hsend, hrecv, h_recv_sem)
+    keep_own(me_ctx, gsend, grecv, g_recv_sem)
+    keep_own(me_ctx, xsend, xrecv, x_recv_sem)
+    loads[4].wait()
 
     arrive(hrecv, h_recv_sem)
-    hwide = hrecv.reshape(n_dp * OWN, LANES)
-
-    @pl.loop(0, OWN)
-    def _(c):
+    hwide[...] = hrecv[...].astype(F32).reshape(n_dp * OWN, LANES)
+    for c in range(OWN):
         build_toeplitz(hwide, toep, c)
 
     arrive(grecv, g_recv_sem)
     widen(grecv, gwide)
-
-    @pl.loop(0, OWN)
-    def _(c):
+    for c in range(OWN):
         build_windows(gwide, win, c)
+    for c in range(OWN):
         back_rows(toep, win, yall, c)
-
-    finish_back(yall, gwide, gain_ref, me_ctx * OWN, xwide)
+    finish_back(yall, gwide, gain, me_ctx * OWN, xwide)
     for v in range(2):
         ysend[:, :, v * LANES : (v + 1) * LANES] = xwide[v].reshape(16, 16, LANES).astype(BF16)
-    scatter(n_ctx, over_ctx, me_ctx, ysend, yrecv, y_send_sem, y_recv_sem)
+    scatter(0, half, far_ctx, me_ctx, ysend, yrecv, y_send_sem, y_recv_sem)
+    scatter(1, half, near_ctx, me_ctx, ysend, yrecv, y_send_sem, y_recv_sem)
+    keep_own(me_ctx, ysend, yrecv, y_recv_sem)
 
     arrive(xrecv, x_recv_sem)
     widen(xrecv, xwide)
     turn_inputs(xwide, xall)
-    dwide = dsend.reshape(n_dp * OWN, LANES)
-
-    @pl.loop(0, OWN)
-    def _(c):
+    for c in range(OWN):
         filter_rows(xall, xs, win, dwide, c)
-
-    scatter(n_dp, over_dp, me_dp, dsend, grad_ref, d_send_sem, d_recv_sem)
-
-    arrive(yrecv, y_recv_sem)
-    back = yrecv[...].astype(F32)
-    for s in range(SEQ):
-        wide[pl.ds(s, 256, stride=2), :] = back[:, s * OWN : (s + 1) * OWN, :].reshape(16 * OWN, 256).T
-    out_ref[...] = wide[...].astype(BF16)
-
-    arrive(grad_ref, d_recv_sem)
-    sent(n_dp, filt_ref, h_send_sem)
+    dsend[...] = dwide[...].reshape(n_dp, OWN, LANES).astype(BF16)
+    scatter(1, n_dp, over_dp, me_dp, dsend, drecv, d_send_sem, d_recv_sem)
+    keep_own(me_dp, dsend, drecv, d_recv_sem)
+
+    sent(n_dp, hsend, h_send_sem)
     sent(n_ctx, gsend, g_send_sem)
     sent(n_ctx, xsend, x_send_sem)
     sent(n_ctx, ysend, y_send_sem)
     sent(n_dp, dsend, d_send_sem)
+    arrive(yrecv, y_recv_sem)
+    arrive(drecv, d_recv_sem)
+
+
+def finish_kernel(yrecv, drecv, out_ref, grad_ref, y_in, d_in, wide, out, grad, load_sem):
+    loads = [
+        pltpu.make_async_copy(src, dst, load_sem.at[n])
+        for n, (src, dst) in enumerate(((drecv, d_in), (yrecv, y_in)))
+    ]
+    stores = [
+        pltpu.make_async_copy(src, dst, load_sem.at[n])
+        for n, (src, dst) in enumerate(((grad, grad_ref), (out, out_ref)))
+    ]
+    for load in loads:
+        load.start()
+    loads[0].wait()
+    grad[...] = d_in[...].astype(F32)
+    stores[0].start()
+    loads[1].wait()
+    back = y_in[...].astype(F32)
+    for s in range(SEQ):
+        wide[pl.ds(s, 256, stride=2), :] = back[:, s * OWN : (s + 1) * OWN, :].reshape(16 * OWN, 256).T
+    out[...] = wide[...].astype(BF16)
+    stores[1].start()
+    for store in stores:
+        store.wait()
 
 
 def body(upstream, gate_value, conv_input, filters, skip_gain):
@@ -275,38 +320,42 @@
     n_dp = lax.axis_size("dp")
     rows = upstream.shape[0] * upstream.shape[1]
     width = upstream.shape[2]
-    vmem = pl.BlockSpec(memory_space=pltpu.VMEM)
     block = (16, 16, 256)
+    hbm = pl.BlockSpec(memory_space=pltpu.HBM)
+    grant = 56 * 1024 * 1024
     back, grads = pl.pallas_call(
         functools.partial(kernel, n_ctx, n_dp),
-        out_shape=(
-            jax.ShapeDtypeStruct((rows, width), BF16),
-            jax.ShapeDtypeStruct(filters.shape, F32),
-        ),
-        in_specs=[vmem, vmem, vmem, pl.BlockSpec(memory_space=pltpu.VMEM), pl.BlockSpec(memory_space=pltpu.SMEM)],
-        out_specs=(vmem, vmem),
+        out_shape=(jax.ShapeDtypeStruct(block, BF16), jax.ShapeDtypeStruct(filters.shape, BF16)),
+        in_specs=[hbm] * 5,
+        out_specs=[hbm] * 2,
         scratch_shapes=[
+            pltpu.VMEM((rows, width), BF16),
+            pltpu.VMEM((rows, width), BF16),
+            pltpu.VMEM((rows, width), BF16),
+            pltpu.VMEM(filters.shape, F32),
+            pltpu.SMEM(skip_gain.shape, F32),
             pltpu.VMEM((rows, width), F32),
             pltpu.VMEM(block, BF16),
             pltpu.VMEM(block, BF16),
-            pltpu.VMEM(block, BF16),
-            pltpu.VMEM(block, BF16),
-            pltpu.VMEM(filters.shape, F32),
+            pltpu.VMEM(filters.shape, BF16),
+            pltpu.VMEM(block, BF16),
+            pltpu.VMEM(block, BF16),
+            pltpu.VMEM(filters.shape, BF16),
             pltpu.VMEM((2, 256, LANES), F32),
             pltpu.VMEM((2, 256, LANES), F32),
+            pltpu.VMEM((n_dp * OWN, LANES), F32),
             pltpu.VMEM((OWN, 8 * HOP, SPAN), BF16),
             pltpu.VMEM((OWN, SPAN, SPAN), BF16),
             pltpu.VMEM((OWN * HOP, SPAN), F32),
             pltpu.VMEM(block, BF16),
-            pltpu.VMEM(block, BF16),
             pltpu.VMEM((OWN * HOP, SPAN), F32),
             pltpu.VMEM((8 * HOP, SPAN), BF16),
-            pltpu.VMEM(filters.shape, F32),
+            pltpu.VMEM((n_dp * OWN, LANES), F32),
+            pltpu.VMEM(filters.shape, BF16),
         ]
+        + [pltpu.SemaphoreType.DMA((5,))]
         + [pltpu.SemaphoreType.DMA] * 10,
-        compiler_params=pltpu.CompilerParams(
-            collective_id=0, has_side_effects=True, vmem_limit_bytes=32 * 1024 * 1024
-        ),
+        compiler_params=pltpu.CompilerParams(collective_id=0, has_side_effects=True, vmem_limit_bytes=grant),
     )(
         upstream.reshape(rows, width),
         gate_value.reshape(rows, width),
@@ -314,7 +363,22 @@
         filters,
         skip_gain,
     )
-    return back.reshape(upstream.shape), grads
+    out, grad = pl.pallas_call(
+        finish_kernel,
+        out_shape=(jax.ShapeDtypeStruct((rows, width), BF16), jax.ShapeDtypeStruct(filters.shape, F32)),
+        in_specs=[hbm] * 2,
+        out_specs=[hbm] * 2,
+        scratch_shapes=[
+            pltpu.VMEM(block, BF16),
+            pltpu.VMEM(filters.shape, BF16),
+            pltpu.VMEM((rows, width), F32),
+            pltpu.VMEM((rows, width), BF16),
+            pltpu.VMEM(filters.shape, F32),
+            pltpu.SemaphoreType.DMA((2,)),
+        ],
+        compiler_params=pltpu.CompilerParams(vmem_limit_bytes=grant),
+    )(back, grads)
+    return out.reshape(upstream.shape), grad
 
 
 def solution(mesh):

time: 48.5 us -> 38.1 us (0.79)
  local copies, waits for them, and re-layouts: 5.58 us -> 0 us
  Pallas kernels: 42.1 us -> 37.3 us
    pallas_call x1, Pallas kernels: 42.1 us -> 35.5 us  [body(): pl.pallas_call(functools.partial(kernel, n_ctx, n_dp), out_shape=(jax.Sha...]
    unnamed x12 -> x0, local copies, waits for them, and re-layouts: 5.58 us -> none
    pallas_call x0 -> x1, Pallas kernels: none -> 1.74 us  [body(): pl.pallas_call(finish_kernel, out_shape=(jax.ShapeDtypeStruct((rows, widt...]
where the time goes in v2:
time: 38.1 us; the launch traced here: 37.9 us
  Pallas kernels  37.3 us (98%)
  between operations  0.64 us (2%)
    pallas_call x1, Pallas kernels, body(): pl.pallas_call(functools.partial(kernel, n_ctx, n_dp), out_shape=(jax.Sha...  35.5 us
    pallas_call x1, Pallas kernels, body(): pl.pallas_call(finish_kernel, out_shape=(jax.ShapeDtypeStruct((rows, widt...  1.74 us

profile of v2, /device:TPU:1, one launch (start us, length us, event | category | flops | bytes accessed | tf_op | source)
XLA Modules:
  0.0 37.9 jit_solution(4538166673372792088)
XLA Ops:
  0.6 35.5 %shard_map.68 = (bf16[16,16,256]{2,1,0:T(8,128)(2,1)}, bf16[32,8,128]{2,1,0:T(8,128)(2,1)}) custom-call(bf16[512,128]{1,0:T(8,128)(2,1)} %bitcast.4, bf16[512,128]{1,0:T(8,128)(2,1)} %bitcast.5, bf16[512,128]{1,0:T(8,128)(2,1)} %bitcast.6, f32[32,8,128]{2,1,0:T(8,128)} %filt_ref.1, f32[128]{0:T(128)} %gain_ref.1), custom_call_target="tpu_custom_call" | custom-call | tf_op jit(solution)/shard_map/pallas_call | solution.py:326
  36.2 1.7 %shard_map.69 = (bf16[512,128]{1,0:T(8,128)(2,1)}, f32[32,8,128]{2,1,0:T(8,128)}) custom-call(bf16[16,16,256]{2,1,0:T(8,128)(2,1)} %get-tuple-element.6.yrecv, bf16[32,8,128]{2,1,0:T(8,128)(2,1)} %get-tuple-element.7.drecv), custom_call_target="tpu_custom_call" | custom-call | tf_op jit(solution)/shard_map/pallas_call | solution.py:366

commit v3 on v2

--- a/solution.py
+++ b/solution.py
@@ -16,6 +16,7 @@
 LANES = 128
 OWN = 8
 SEQ = 2
+LINE = 8
 
 
 def lane_index(shape):
@@ -168,13 +169,13 @@
 
 
 def kernel(
-    n_ctx, n_dp,
+    n_ctx, n_dp, n_y,
     up_ref, gate_ref, in_ref, filt_ref, gain_ref,
     yrecv, drecv,
-    up, gate, raw, filt, gain, wide, gsend, xsend, hsend, grecv, xrecv, hrecv, gwide, xwide, hwide, toep, win,
-    yall, ysend, xall, xs, dwide, dsend,
+    up, gate, raw, filt, gain, wide, gsend, xsend, hsend, hpass, hturn, grecv, xrecv, hrecv, gwide, xwide, hwide, toep, win,
+    yall, ywide, ysend, xall, xs, dwide, dsend,
     load_sem,
-    h_send_sem, h_recv_sem, g_send_sem, g_recv_sem, x_send_sem, x_recv_sem,
+    h_send_sem, h_recv_sem, t_send_sem, t_recv_sem, g_send_sem, g_recv_sem, x_send_sem, x_recv_sem,
     y_send_sem, y_recv_sem, d_send_sem, d_recv_sem,
 ):
     me_ctx = lax.axis_index("ctx")
@@ -182,6 +183,9 @@
     half = n_ctx // 2
     me_hi = me_ctx // half
     me_lo = lax.rem(me_ctx, half)
+    n_z = n_dp // n_y
+    me_z = me_dp // n_y
+    me_y = lax.rem(me_dp, n_y)
 
     def far_ctx(step):
         peer = (1 - me_hi) * half + lax.rem(me_lo + step, half)
@@ -194,6 +198,14 @@
     def over_dp(step):
         peer = lax.rem(me_dp + step, n_dp)
         return peer, {"ctx": me_ctx, "dp": peer}
+
+    def over_y(step):
+        peer = lax.rem(me_y + step, n_y)
+        return peer, {"ctx": me_ctx, "dp": me_z * n_y + peer}
+
+    def over_z(step):
+        peer = lax.rem(me_z + step, n_z)
+        return peer, {"ctx": me_ctx, "dp": peer * n_y + me_y}
 
     loads = [
         pltpu.make_async_copy(src, dst, load_sem.at[n])
@@ -212,7 +224,8 @@
             pl.semaphore_signal(barrier, inc=1, device_id=over(step)[1], device_id_type=MESH)
 
     greet(0, half, far_ctx)
-    greet(1, n_dp, over_dp)
+    greet(1, n_y, over_y)
+    greet(1, n_z, over_z)
     greet(1, half, near_ctx)
 
     def scatter(first, last, over, me, src, dst, send_sem, recv_sem):
@@ -239,50 +252,74 @@
     wide[...] = (up[...].astype(F32) * gate[...].astype(F32)).astype(BF16).astype(F32)
     spread_rows(wide, gsend)
     loads[3].wait()
-    hsend[...] = filt[...].astype(BF16)
+    lags = filt[...].reshape(n_z, n_y, OWN, LANES)
+    hsend[...] = jnp.swapaxes(lags, 0, 1).reshape(n_y, n_z * OWN, LANES).astype(BF16)
     loads[2].wait()
     wide[...] = raw[...].astype(F32)
     spread_rows(wide, xsend)
 
-    pl.semaphore_wait(barrier, n_ctx + n_dp - 2)
+    pl.semaphore_wait(barrier, n_ctx + n_y + n_z - 3)
     scatter(0, half, far_ctx, me_ctx, gsend, grecv, g_send_sem, g_recv_sem)
-    scatter(1, n_dp, over_dp, me_dp, hsend, hrecv, h_send_sem, h_recv_sem)
+
+    @pl.when(me_hi == 1)
+    def _():
+        scatter(0, half, far_ctx, me_ctx, xsend, xrecv, x_send_sem, x_recv_sem)
+
+    scatter(1, n_y, over_y, me_y, hsend, hpass, h_send_sem, h_recv_sem)
     scatter(1, half, near_ctx, me_ctx, gsend, grecv, g_send_sem, g_recv_sem)
-    scatter(0, half, far_ctx, me_ctx, xsend, xrecv, x_send_sem, x_recv_sem)
     scatter(1, half, near_ctx, me_ctx, xsend, xrecv, x_send_sem, x_recv_sem)
-    keep_own(me_dp, hsend, hrecv, h_recv_sem)
+    keep_own(me_y, hsend, hpass, h_recv_sem)
     keep_own(me_ctx, gsend, grecv, g_recv_sem)
     keep_own(me_ctx, xsend, xrecv, x_recv_sem)
     loads[4].wait()
 
-    arrive(hrecv, h_recv_sem)
-    hwide[...] = hrecv[...].astype(F32).reshape(n_dp * OWN, LANES)
-    for c in range(OWN):
-        build_toeplitz(hwide, toep, c)
+    arrive(hpass, h_recv_sem)
+    lags = hpass[...].astype(F32).reshape(n_y, n_z, OWN, LANES)
+    hturn[...] = jnp.swapaxes(lags, 0, 1).reshape(n_z, n_y * OWN, LANES).astype(BF16)
+    scatter(1, n_z, over_z, me_z, hturn, hrecv, t_send_sem, t_recv_sem)
+    keep_own(me_z, hturn, hrecv, t_recv_sem)
 
     arrive(grecv, g_recv_sem)
+
+    @pl.when(me_hi == 0)
+    def _():
+        scatter(0, half, far_ctx, me_ctx, xsend, xrecv, x_send_sem, x_recv_sem)
+
     widen(grecv, gwide)
     for c in range(OWN):
         build_windows(gwide, win, c)
-    for c in range(OWN):
-        back_rows(toep, win, yall, c)
-    finish_back(yall, gwide, gain, me_ctx * OWN, xwide)
-    for v in range(2):
-        ysend[:, :, v * LANES : (v + 1) * LANES] = xwide[v].reshape(16, 16, LANES).astype(BF16)
-    scatter(0, half, far_ctx, me_ctx, ysend, yrecv, y_send_sem, y_recv_sem)
-    scatter(1, half, near_ctx, me_ctx, ysend, yrecv, y_send_sem, y_recv_sem)
-    keep_own(me_ctx, ysend, yrecv, y_recv_sem)
-
-    arrive(xrecv, x_recv_sem)
-    widen(xrecv, xwide)
-    turn_inputs(xwide, xall)
-    for c in range(OWN):
-        filter_rows(xall, xs, win, dwide, c)
-    dsend[...] = dwide[...].reshape(n_dp, OWN, LANES).astype(BF16)
-    scatter(1, n_dp, over_dp, me_dp, dsend, drecv, d_send_sem, d_recv_sem)
-    keep_own(me_dp, dsend, drecv, d_recv_sem)
-
-    sent(n_dp, hsend, h_send_sem)
+
+    @pl.loop(0, 2)
+    def _(turn):
+        @pl.when(turn != me_hi)
+        def _():
+            arrive(hrecv, t_recv_sem)
+            hwide[...] = hrecv[...].astype(F32).reshape(n_dp * OWN, LANES)
+            for c in range(OWN):
+                build_toeplitz(hwide, toep, c)
+
+            for c in range(OWN):
+                back_rows(toep, win, yall, c)
+            finish_back(yall, gwide, gain, me_ctx * OWN, ywide)
+            for v in range(2):
+                ysend[:, :, v * LANES : (v + 1) * LANES] = ywide[v].reshape(16, 16, LANES).astype(BF16)
+            scatter(0, half, far_ctx, me_ctx, ysend, yrecv, y_send_sem, y_recv_sem)
+            scatter(1, half, near_ctx, me_ctx, ysend, yrecv, y_send_sem, y_recv_sem)
+            keep_own(me_ctx, ysend, yrecv, y_recv_sem)
+
+        @pl.when(turn == me_hi)
+        def _():
+            arrive(xrecv, x_recv_sem)
+            widen(xrecv, xwide)
+            turn_inputs(xwide, xall)
+            for c in range(OWN):
+                filter_rows(xall, xs, win, dwide, c)
+            dsend[...] = dwide[...].reshape(n_dp, OWN, LANES).astype(BF16)
+            scatter(1, n_dp, over_dp, me_dp, dsend, drecv, d_send_sem, d_recv_sem)
+            keep_own(me_dp, dsend, drecv, d_recv_sem)
+
+    sent(n_y, hsend, h_send_sem)
+    sent(n_z, hturn, t_send_sem)
     sent(n_ctx, gsend, g_send_sem)
     sent(n_ctx, xsend, x_send_sem)
     sent(n_ctx, ysend, y_send_sem)
@@ -291,21 +328,13 @@
     arrive(drecv, d_recv_sem)
 
 
-def finish_kernel(yrecv, drecv, out_ref, grad_ref, y_in, d_in, wide, out, grad, load_sem):
-    loads = [
-        pltpu.make_async_copy(src, dst, load_sem.at[n])
-        for n, (src, dst) in enumerate(((drecv, d_in), (yrecv, y_in)))
-    ]
+def finish_kernel(y_in, d_in, out_ref, grad_ref, wide, out, grad, store_sem):
     stores = [
-        pltpu.make_async_copy(src, dst, load_sem.at[n])
+        pltpu.make_async_copy(src, dst, store_sem.at[n])
         for n, (src, dst) in enumerate(((grad, grad_ref), (out, out_ref)))
     ]
-    for load in loads:
-        load.start()
-    loads[0].wait()
     grad[...] = d_in[...].astype(F32)
     stores[0].start()
-    loads[1].wait()
     back = y_in[...].astype(F32)
     for s in range(SEQ):
         wide[pl.ds(s, 256, stride=2), :] = back[:, s * OWN : (s + 1) * OWN, :].reshape(16 * OWN, 256).T
@@ -318,16 +347,18 @@
 def body(upstream, gate_value, conv_input, filters, skip_gain):
     n_ctx = lax.axis_size("ctx")
     n_dp = lax.axis_size("dp")
+    n_y = LINE
+    n_z = n_dp // n_y
     rows = upstream.shape[0] * upstream.shape[1]
     width = upstream.shape[2]
     block = (16, 16, 256)
     hbm = pl.BlockSpec(memory_space=pltpu.HBM)
     grant = 56 * 1024 * 1024
     back, grads = pl.pallas_call(
-        functools.partial(kernel, n_ctx, n_dp),
-        out_shape=(jax.ShapeDtypeStruct(block, BF16), jax.ShapeDtypeStruct(filters.shape, BF16)),
+        functools.partial(kernel, n_ctx, n_dp, n_y),
+        out_shape=(pltpu.VMEM(block, BF16), pltpu.VMEM(filters.shape, BF16)),
         in_specs=[hbm] * 5,
-        out_specs=[hbm] * 2,
+        out_specs=[pl.BlockSpec(memory_space=pltpu.VMEM)] * 2,
         scratch_shapes=[
             pltpu.VMEM((rows, width), BF16),
             pltpu.VMEM((rows, width), BF16),
@@ -337,16 +368,19 @@
             pltpu.VMEM((rows, width), F32),
             pltpu.VMEM(block, BF16),
             pltpu.VMEM(block, BF16),
-            pltpu.VMEM(filters.shape, BF16),
+            pltpu.VMEM((n_y, n_z * OWN, LANES), BF16),
+            pltpu.VMEM((n_y, n_z * OWN, LANES), BF16),
+            pltpu.VMEM((n_z, n_y * OWN, LANES), BF16),
             pltpu.VMEM(block, BF16),
             pltpu.VMEM(block, BF16),
-            pltpu.VMEM(filters.shape, BF16),
+            pltpu.VMEM((n_z, n_y * OWN, LANES), BF16),
             pltpu.VMEM((2, 256, LANES), F32),
             pltpu.VMEM((2, 256, LANES), F32),
             pltpu.VMEM((n_dp * OWN, LANES), F32),
             pltpu.VMEM((OWN, 8 * HOP, SPAN), BF16),
             pltpu.VMEM((OWN, SPAN, SPAN), BF16),
             pltpu.VMEM((OWN * HOP, SPAN), F32),
+            pltpu.VMEM((2, 256, LANES), F32),
             pltpu.VMEM(block, BF16),
             pltpu.VMEM((OWN * HOP, SPAN), F32),
             pltpu.VMEM((8 * HOP, SPAN), BF16),
@@ -354,7 +388,7 @@
             pltpu.VMEM(filters.shape, BF16),
         ]
         + [pltpu.SemaphoreType.DMA((5,))]
-        + [pltpu.SemaphoreType.DMA] * 10,
+        + [pltpu.SemaphoreType.DMA] * 12,
         compiler_params=pltpu.CompilerParams(collective_id=0, has_side_effects=True, vmem_limit_bytes=grant),
     )(
         upstream.reshape(rows, width),
@@ -366,17 +400,15 @@
     out, grad = pl.pallas_call(
         finish_kernel,
         out_shape=(jax.ShapeDtypeStruct((rows, width), BF16), jax.ShapeDtypeStruct(filters.shape, F32)),
-        in_specs=[hbm] * 2,
+        in_specs=[pl.BlockSpec(memory_space=pltpu.VMEM)] * 2,
         out_specs=[hbm] * 2,
         scratch_shapes=[
-            pltpu.VMEM(block, BF16),
-            pltpu.VMEM(filters.shape, BF16),
             pltpu.VMEM((rows, width), F32),
             pltpu.VMEM((rows, width), BF16),
             pltpu.VMEM(filters.shape, F32),
             pltpu.SemaphoreType.DMA((2,)),
         ],
-        compiler_params=pltpu.CompilerParams(vmem_limit_bytes=grant),
+        compiler_params=pltpu.CompilerParams(vmem_limit_bytes=16 * 1024 * 1024),
     )(back, grads)
     return out.reshape(upstream.shape), grad
 

time: 38.1 us -> 34.3 us (0.900)
  Pallas kernels: 37.3 us -> 33.5 us
    pallas_call x1, Pallas kernels: 35.5 us -> 32.7 us  [body(): pl.pallas_call(functools.partial(kernel, n_ctx, n_dp, n_y), out_shape=(pl...]
    pallas_call x1, Pallas kernels: 1.74 us -> 0.8 us  [body(): pl.pallas_call(finish_kernel, out_shape=(jax.ShapeDtypeStruct((rows, widt...]
where the time goes in v3:
time: 34.3 us; the launch traced here: 34.1 us
  Pallas kernels  33.5 us (98%)
  between operations  0.64 us (2%)
    pallas_call x1, Pallas kernels, body(): pl.pallas_call(functools.partial(kernel, n_ctx, n_dp, n_y), out_shape=(pl...  32.7 us
    pallas_call x1, Pallas kernels, body(): pl.pallas_call(finish_kernel, out_shape=(jax.ShapeDtypeStruct((rows, widt...  0.8 us

profile of v3, /device:TPU:1, one launch (start us, length us, event | category | flops | bytes accessed | tf_op | source)
XLA Modules:
  0.0 34.1 jit_solution(2117254185926464485)
XLA Ops:
  0.6 32.7 %shard_map.68 = (bf16[16,16,256]{2,1,0:T(8,128)(2,1)S(1)}, bf16[32,8,128]{2,1,0:T(8,128)(2,1)S(1)}) custom-call(bf16[512,128]{1,0:T(8,128)(2,1)} %bitcast.4, bf16[512,128]{1,0:T(8,128)(2,1)} %bitcast.5, bf16[512,128]{1,0:T(8,128)(2,1)} %bitcast.6, f32[32,8,128]{2,1,0:T(8,128)} %filt_ref.1, f32[128]{0:T(128)} %gain_ref.1), custom_call_target="tpu_custom_call" | custom-call | tf_op jit(solution)/shard_map/pallas_call | solution.py:357
  33.4 0.8 %shard_map.69 = (bf16[512,128]{1,0:T(8,128)(2,1)}, f32[32,8,128]{2,1,0:T(8,128)}) custom-call(bf16[16,16,256]{2,1,0:T(8,128)(2,1)S(1)} %get-tuple-element.6.y_in, bf16[32,8,128]{2,1,0:T(8,128)(2,1)S(1)} %get-tuple-element.7.d_in), custom_call_target="tpu_custom_call" | custom-call | tf_op jit(solution)/shard_map/pallas_call | solution.py:400

commit v4 on v3

--- a/solution.py
+++ b/solution.py
@@ -91,37 +91,32 @@
             win_ref[c, j * 16 : (j + 1) * 16, :] = turned[:, LANES * jt : LANES * jt + SPAN].astype(BF16)
 
 
-def back_rows(toep_ref, win_ref, yall_ref, c):
-    out = lax.dot_general(
-        toep_ref[c], win_ref[c], (((1,), (1,)), ((), ())), preferred_element_type=F32
-    )
+def back_rows(toep_ref, wint_ref, yall_ref, c, h):
+    out = jnp.dot(toep_ref[c], wint_ref[c, :, 256 * h : 256 * h + 256], preferred_element_type=F32)
     group = lane_index((HOP, LANES)) % 8
-    cols = []
-    for n in range(4):
+    for n in range(2):
         tile = out[:, n * LANES : (n + 1) * LANES]
         total = tile[0:HOP]
         for q in range(1, 8):
             turned = pltpu.roll(tile[q * HOP : (q + 1) * HOP], LANES - q, 1)
             total = total + jnp.where(group < 8 - q, turned, 0.0)
-        cols.append(total)
-    yall_ref[pl.ds(pl.multiple_of(c * HOP, HOP), HOP), :] = jnp.concatenate(cols, axis=1)
-
-
-def finish_back(yall_ref, gwide_ref, gain_ref, first_gain, ywide_ref):
+        yall_ref[c * HOP : (c + 1) * HOP, 256 * h + n * LANES : 256 * h + (n + 1) * LANES] = total
+
+
+def finish_back(yall_ref, gwide_ref, gain_ref, first_gain, ywide_ref, ysend_ref, h):
     cols = []
-    for n in range(4):
+    for n in (2 * h, 2 * h + 1):
         turned = yall_ref[:, n * LANES : (n + 1) * LANES].T
         cols.append(swap_groups([turned[HOP * r : HOP * (r + 1)] for r in range(8)]))
     for c in range(OWN):
-        rows = jnp.concatenate([cols[n][c] for n in range(4)], axis=1)
-        rows = rows + gain_ref[first_gain + c] * own_rows(gwide_ref, c)
-        for s in range(SEQ):
-            for h in range(2):
-                for v in range(2):
-                    n = 2 * h + v
-                    ywide_ref[v, pl.ds(h * 16 + s * OWN + c, 8, stride=32), :] = rows[
-                        8 * s : 8 * s + 8, n * LANES : (n + 1) * LANES
-                    ]
+        gain = gain_ref[first_gain + c]
+        for v in range(2):
+            for s in range(SEQ):
+                rows = cols[v][c][8 * s : 8 * s + 8]
+                here = gwide_ref[v, pl.ds(h * 16 + s * OWN + c, 8, stride=32), :]
+                ywide_ref[v, pl.ds(s * OWN + c, 8, stride=16), :] = rows + gain * here
+    for v in range(2):
+        ysend_ref[:, h, :, v * LANES : (v + 1) * LANES] = ywide_ref[v].reshape(8, 16, LANES).astype(BF16)
 
 
 def turn_inputs(xwide_ref, xall_ref):
@@ -131,27 +126,25 @@
         xall_ref[:, n * LANES : (n + 1) * LANES] = jnp.concatenate(blocks, axis=0).T
 
 
-def filter_rows(xall_ref, xs_ref, win_ref, dwide_ref, c):
-    keep = (lane_index((8, LANES)) % 8) >= row_index((8, LANES))
-    for pair in range(8):
-        rows = []
-        for a in (2 * pair, 2 * pair + 1):
-            line = xall_ref[pl.ds(c * HOP + a, 1), :]
-            tiles = []
-            for n in range(4):
-                wide = jnp.broadcast_to(line[:, n * LANES : (n + 1) * LANES], (8, LANES))
-                turned = pltpu.roll(wide, 0, 1, stride=1, stride_axis=0)
-                tiles.append(jnp.where(keep, turned, 0.0))
-            rows.append(jnp.concatenate(tiles, axis=1))
-        xs_ref[pair * 16 : (pair + 1) * 16, :] = jnp.concatenate(rows, axis=0).astype(BF16)
-    out = jnp.dot(xs_ref[...], win_ref[c], preferred_element_type=F32)
+def shift_inputs(xall_ref, xs_ref, c):
+    group = lane_index((HOP, LANES)) % 8
+    for n in range(4):
+        tile = xall_ref[c * HOP : (c + 1) * HOP, n * LANES : (n + 1) * LANES].astype(BF16)
+        for q in range(8):
+            turned = tile if q == 0 else jnp.where(group >= q, pltpu.roll(tile, q, 1), jnp.zeros_like(tile))
+            xs_ref[c, q * HOP : (q + 1) * HOP, n * LANES : (n + 1) * LANES] = turned
+
+
+def filter_rows(xs_ref, win_ref, sums_ref, dwide_ref, c):
+    out = jnp.dot(xs_ref[c], win_ref[c], preferred_element_type=F32)
+    for n in range(4):
+        sums_ref[c, n] = out[:, n * LANES : (n + 1) * LANES]
     lane = lane_index((8, LANES))
-    sums = [out[0:8, n * LANES : (n + 1) * LANES] for n in range(4)]
+    rows = [[sums_ref[c, n, pl.ds(a, 8, stride=HOP), :] for n in range(4)] for a in range(HOP)]
+    sums = rows[0]
     wrapped = jnp.zeros((8, LANES), F32)
     for a in range(1, HOP):
-        turned = [
-            pltpu.roll(out[8 * a : 8 * a + 8, n * LANES : (n + 1) * LANES], LANES - a, 1) for n in range(4)
-        ]
+        turned = [pltpu.roll(row, LANES - a, 1) for row in rows[a]]
         inside = lane < LANES - a
         for n in range(3):
             sums[n] = sums[n] + jnp.where(inside, turned[n], turned[n + 1])
@@ -172,9 +165,9 @@
     n_ctx, n_dp, n_y,
     up_ref, gate_ref, in_ref, filt_ref, gain_ref,
     yrecv, drecv,
-    up, gate, raw, filt, gain, wide, gsend, xsend, hsend, hpass, hturn, grecv, xrecv, hrecv, gwide, xwide, hwide, toep, win,
-    yall, ywide, ysend, xall, xs, dwide, dsend,
-    load_sem,
+    up, gate, raw, filt, gain, wide, gsend, xsend, hsend, hpass, grecv, xrecv, hrecv, gwide, xwide, hwide, toep, win, wint,
+    yall, ywide, ysend, xall, xs, sums, dwide, dsend,
+    hello, hello_z, load_sem,
     h_send_sem, h_recv_sem, t_send_sem, t_recv_sem, g_send_sem, g_recv_sem, x_send_sem, x_recv_sem,
     y_send_sem, y_recv_sem, d_send_sem, d_recv_sem,
 ):
@@ -199,6 +192,9 @@
         peer = lax.rem(me_dp + step, n_dp)
         return peer, {"ctx": me_ctx, "dp": peer}
 
+    def to_dp(peer):
+        return peer, {"ctx": me_ctx, "dp": peer}
+
     def over_y(step):
         peer = lax.rem(me_y + step, n_y)
         return peer, {"ctx": me_ctx, "dp": me_z * n_y + peer}
@@ -207,15 +203,22 @@
         peer = lax.rem(me_z + step, n_z)
         return peer, {"ctx": me_ctx, "dp": peer * n_y + me_y}
 
-    loads = [
-        pltpu.make_async_copy(src, dst, load_sem.at[n])
-        for n, (src, dst) in enumerate(
-            ((up_ref, up), (gate_ref, gate), (in_ref, raw), (filt_ref, filt), (gain_ref, gain))
-        )
-    ]
-    for load in loads:
-        load.start()
-
+    def pieces(src, dst, sem, count):
+        size = dst.shape[0] // count
+        return [
+            pltpu.make_async_copy(src.at[pl.ds(n * size, size)], dst.at[pl.ds(n * size, size)], sem)
+            for n in range(count)
+        ]
+
+    def load(n, src, dst, count=4):
+        for piece in pieces(src, dst, load_sem.at[n], count):
+            piece.start()
+
+    def loaded(n, dst):
+        pltpu.make_async_copy(dst, dst, load_sem.at[n]).wait()
+
+    load(0, up_ref, up)
+    load(1, gate_ref, gate)
     barrier = pltpu.get_barrier_semaphore()
 
     def greet(first, last, over):
@@ -224,8 +227,39 @@
             pl.semaphore_signal(barrier, inc=1, device_id=over(step)[1], device_id_type=MESH)
 
     greet(0, half, far_ctx)
-    greet(1, n_y, over_y)
-    greet(1, n_z, over_z)
+    def edge(y):
+        return jnp.minimum(y, n_y - y)
+
+    def sooner(step):
+        return edge(lax.rem(me_y + step, n_y)) < edge(me_y)
+
+    @pl.when(me_hi == 0)
+    def _():
+        greet(1, n_dp, over_dp)
+
+    @pl.when(me_hi == 1)
+    def _():
+        greet(1, 3, over_y)
+        greet(n_y - 2, n_y, over_y)
+        for step in range(3, n_y - 2):
+            peer, where = over_y(step)
+
+            @pl.when(edge(me_y) < edge(peer))
+            def _():
+                pl.semaphore_signal(barrier, inc=1, device_id=where, device_id_type=MESH)
+
+        for z in range(n_z):
+            where = {"ctx": me_ctx, "dp": z * n_y + me_y}
+
+            @pl.when(jnp.logical_and(z >= me_z - 1, z != me_z))
+            def _():
+                pl.semaphore_signal(barrier, inc=1, device_id=where, device_id_type=MESH)
+
+    heard = 4 + me_z + jnp.where(me_z < n_z - 1, 1, 0)
+    for step in range(3, n_y - 2):
+        heard = heard + jnp.where(sooner(step), 1, 0)
+    greeted = n_ctx - 1 + jnp.where(me_hi == 1, heard, n_dp - 1)
+
     greet(1, half, near_ctx)
 
     def scatter(first, last, over, me, src, dst, send_sem, recv_sem):
@@ -240,6 +274,17 @@
     def keep_own(me, src, dst, recv_sem):
         pltpu.make_async_copy(src.at[me], dst.at[me], recv_sem).start()
 
+    def pass_on(origin, src):
+        pltpu.make_async_copy(src.at[origin, me_z], hrecv.at[me_z, origin], t_recv_sem).start()
+
+        @pl.loop(1, n_z)
+        def _(step):
+            peer, where = over_z(step)
+            pltpu.make_async_remote_copy(
+                src_ref=src.at[origin, peer], dst_ref=hrecv.at[me_z, origin], send_sem=t_send_sem,
+                recv_sem=t_recv_sem, device_id=where, device_id_type=MESH,
+            ).start()
+
     def arrive(dst, sem):
         pltpu.make_async_copy(dst, dst, sem).wait()
 
@@ -247,37 +292,88 @@
         part = src.at[pl.ds(0, count - 1)]
         pltpu.make_async_copy(part, part, sem).wait()
 
-    loads[0].wait()
-    loads[1].wait()
+    load(2, in_ref, raw)
+    load(3, filt_ref, filt)
+    load(4, gain_ref, gain, 1)
+    loaded(0, up)
+    loaded(1, gate)
     wide[...] = (up[...].astype(F32) * gate[...].astype(F32)).astype(BF16).astype(F32)
     spread_rows(wide, gsend)
-    loads[3].wait()
-    lags = filt[...].reshape(n_z, n_y, OWN, LANES)
-    hsend[...] = jnp.swapaxes(lags, 0, 1).reshape(n_y, n_z * OWN, LANES).astype(BF16)
-    loads[2].wait()
+    pl.semaphore_wait(barrier, greeted)
+    scatter(0, half, far_ctx, me_ctx, gsend, grecv, g_send_sem, g_recv_sem)
+    @pl.when(me_hi == 1)
+    def _():
+        for step in (2, n_y - 2):
+            pl.semaphore_signal(hello, inc=1, device_id=over_y(step)[1], device_id_type=MESH)
+        for z in range(n_z - 2):
+
+            @pl.when(z < me_z - 1)
+            def _():
+                pl.semaphore_signal(
+                    hello_z, inc=1, device_id={"ctx": me_ctx, "dp": z * n_y + me_y}, device_id_type=MESH
+                )
+
+    loaded(3, filt)
+    for z in range(n_z):
+        hsend[:, z] = filt[z * n_y : (z + 1) * n_y].astype(BF16)
+    @pl.when(me_hi == 0)
+    def _():
+        pltpu.make_async_copy(hsend.at[me_y, me_z], hrecv.at[me_z, me_y], t_recv_sem).start()
+
+        @pl.loop(1, n_dp)
+        def _(step):
+            peer, where = over_dp(step)
+            pltpu.make_async_remote_copy(
+                src_ref=hsend.at[lax.rem(peer, n_y), peer // n_y], dst_ref=hrecv.at[me_z, me_y],
+                send_sem=t_send_sem, recv_sem=t_recv_sem, device_id=where, device_id_type=MESH,
+            ).start()
+
+    @pl.when(me_hi == 1)
+    def _():
+        scatter(1, 3, over_y, me_y, hsend, hpass, h_send_sem, h_recv_sem.at[0])
+        scatter(n_y - 2, n_y, over_y, me_y, hsend, hpass, h_send_sem, h_recv_sem.at[0])
+        for step in range(3, n_y - 2):
+
+            @pl.when(sooner(step))
+            def _():
+                scatter(step, step + 1, over_y, me_y, hsend, hpass, h_send_sem, h_recv_sem.at[1])
+
+    loaded(2, raw)
     wide[...] = raw[...].astype(F32)
     spread_rows(wide, xsend)
 
-    pl.semaphore_wait(barrier, n_ctx + n_y + n_z - 3)
-    scatter(0, half, far_ctx, me_ctx, gsend, grecv, g_send_sem, g_recv_sem)
-
     @pl.when(me_hi == 1)
     def _():
         scatter(0, half, far_ctx, me_ctx, xsend, xrecv, x_send_sem, x_recv_sem)
 
-    scatter(1, n_y, over_y, me_y, hsend, hpass, h_send_sem, h_recv_sem)
     scatter(1, half, near_ctx, me_ctx, gsend, grecv, g_send_sem, g_recv_sem)
     scatter(1, half, near_ctx, me_ctx, xsend, xrecv, x_send_sem, x_recv_sem)
-    keep_own(me_y, hsend, hpass, h_recv_sem)
     keep_own(me_ctx, gsend, grecv, g_recv_sem)
     keep_own(me_ctx, xsend, xrecv, x_recv_sem)
-    loads[4].wait()
-
-    arrive(hpass, h_recv_sem)
-    lags = hpass[...].astype(F32).reshape(n_y, n_z, OWN, LANES)
-    hturn[...] = jnp.swapaxes(lags, 0, 1).reshape(n_z, n_y * OWN, LANES).astype(BF16)
-    scatter(1, n_z, over_z, me_z, hturn, hrecv, t_send_sem, t_recv_sem)
-    keep_own(me_z, hturn, hrecv, t_recv_sem)
+    loaded(4, gain)
+    @pl.when(me_hi == 1)
+    def _():
+        pl.semaphore_wait(hello, 2)
+        for step in range(3, n_y - 2):
+
+            @pl.when(jnp.logical_not(sooner(step)))
+            def _():
+                scatter(step, step + 1, over_y, me_y, hsend, hpass, h_send_sem, h_recv_sem.at[1])
+
+
+        for z in range(n_z - 2):
+
+            @pl.when(z == me_z)
+            def _():
+                pl.semaphore_wait(hello_z, n_z - 2 - z)
+
+        pass_on(me_y, hsend)
+        arrive(hpass.at[pl.ds(0, 4)], h_recv_sem.at[0])
+        for step in (1, n_y - 1, 2, n_y - 2):
+            pass_on(lax.rem(me_y + step, n_y), hpass)
+        arrive(hpass.at[pl.ds(0, n_y - 5)], h_recv_sem.at[1])
+        for step in range(3, n_y - 2):
+            pass_on(lax.rem(me_y + step, n_y), hpass)
 
     arrive(grecv, g_recv_sem)
 
@@ -288,6 +384,8 @@
     widen(grecv, gwide)
     for c in range(OWN):
         build_windows(gwide, win, c)
+    for c in range(OWN):
+        wint[c] = win[c].T
 
     @pl.loop(0, 2)
     def _(turn):
@@ -298,14 +396,26 @@
             for c in range(OWN):
                 build_toeplitz(hwide, toep, c)
 
-            for c in range(OWN):
-                back_rows(toep, win, yall, c)
-            finish_back(yall, gwide, gain, me_ctx * OWN, ywide)
-            for v in range(2):
-                ysend[:, :, v * LANES : (v + 1) * LANES] = ywide[v].reshape(16, 16, LANES).astype(BF16)
-            scatter(0, half, far_ctx, me_ctx, ysend, yrecv, y_send_sem, y_recv_sem)
-            scatter(1, half, near_ctx, me_ctx, ysend, yrecv, y_send_sem, y_recv_sem)
-            keep_own(me_ctx, ysend, yrecv, y_recv_sem)
+            for h in range(2):
+                for c in range(OWN):
+                    back_rows(toep, wint, yall, c, h)
+                finish_back(yall, gwide, gain, me_ctx * OWN, ywide.at[h], ysend, h)
+
+                @pl.loop(0, n_ctx // 2)
+                def _(step):
+                    block = half // 2 * (step // (half // 2)) + lax.rem(me_lo // 2 + step, half // 2)
+                    peer = 2 * block + h
+
+                    @pl.when(peer != me_ctx)
+                    def _():
+                        pltpu.make_async_remote_copy(
+                            src_ref=ysend.at[block, h], dst_ref=yrecv.at[me_ctx], send_sem=y_send_sem,
+                            recv_sem=y_recv_sem, device_id={"ctx": peer, "dp": me_dp}, device_id_type=MESH,
+                        ).start()
+
+                    @pl.when(peer == me_ctx)
+                    def _():
+                        pltpu.make_async_copy(ysend.at[block, h], yrecv.at[me_ctx], y_recv_sem).start()
 
         @pl.when(turn == me_hi)
         def _():
@@ -313,35 +423,51 @@
             widen(xrecv, xwide)
             turn_inputs(xwide, xall)
             for c in range(OWN):
-                filter_rows(xall, xs, win, dwide, c)
+                shift_inputs(xall, xs, c)
+            for c in range(OWN):
+                filter_rows(xs, win, sums, dwide, c)
             dsend[...] = dwide[...].reshape(n_dp, OWN, LANES).astype(BF16)
-            scatter(1, n_dp, over_dp, me_dp, dsend, drecv, d_send_sem, d_recv_sem)
+            scatter(0, me_dp, to_dp, me_dp, dsend, drecv, d_send_sem, d_recv_sem)
+            scatter(me_dp + 1, n_dp, to_dp, me_dp, dsend, drecv, d_send_sem, d_recv_sem)
             keep_own(me_dp, dsend, drecv, d_recv_sem)
 
-    sent(n_y, hsend, h_send_sem)
-    sent(n_z, hturn, t_send_sem)
+    @pl.when(me_hi == 0)
+    def _():
+        sent(n_dp, hrecv.reshape(n_dp, OWN, LANES), t_send_sem)
+
+    @pl.when(me_hi == 1)
+    def _():
+        sent(n_y, hsend, h_send_sem)
+        sent(n_z, hrecv, t_send_sem)
+
     sent(n_ctx, gsend, g_send_sem)
     sent(n_ctx, xsend, x_send_sem)
-    sent(n_ctx, ysend, y_send_sem)
+    sent(n_ctx, yrecv, y_send_sem)
     sent(n_dp, dsend, d_send_sem)
     arrive(yrecv, y_recv_sem)
     arrive(drecv, d_recv_sem)
 
 
 def finish_kernel(y_in, d_in, out_ref, grad_ref, wide, out, grad, store_sem):
-    stores = [
-        pltpu.make_async_copy(src, dst, store_sem.at[n])
-        for n, (src, dst) in enumerate(((grad, grad_ref), (out, out_ref)))
-    ]
-    grad[...] = d_in[...].astype(F32)
-    stores[0].start()
-    back = y_in[...].astype(F32)
-    for s in range(SEQ):
-        wide[pl.ds(s, 256, stride=2), :] = back[:, s * OWN : (s + 1) * OWN, :].reshape(16 * OWN, 256).T
-    out[...] = wide[...].astype(BF16)
-    stores[1].start()
-    for store in stores:
-        store.wait()
+    def store(n, src, dst, first, size):
+        part = pl.ds(first, size)
+        pltpu.make_async_copy(src.at[part], dst.at[part], store_sem.at[n]).start()
+
+    for n in range(4):
+        grad[8 * n : 8 * n + 8] = d_in[8 * n : 8 * n + 8].astype(F32)
+        store(0, grad, grad_ref, 8 * n, 8)
+    for n in range(2):
+        time = slice(n * LANES, (n + 1) * LANES)
+        back = y_in[:, :, time].astype(F32)
+        for s in range(SEQ):
+            wide[pl.ds(256 * n + s, LANES, stride=2), :] = (
+                back[:, s * OWN : (s + 1) * OWN, :].reshape(16 * OWN, LANES).T
+            )
+        out[256 * n : 256 * n + 256] = wide[256 * n : 256 * n + 256].astype(BF16)
+        for k in range(2):
+            store(1, out, out_ref, 256 * n + 128 * k, 128)
+    pltpu.make_async_copy(grad, grad_ref, store_sem.at[0]).wait()
+    pltpu.make_async_copy(out, out_ref, store_sem.at[1]).wait()
 
 
 def body(upstream, gate_value, conv_input, filters, skip_gain):
@@ -368,27 +494,30 @@
             pltpu.VMEM((rows, width), F32),
             pltpu.VMEM(block, BF16),
             pltpu.VMEM(block, BF16),
-            pltpu.VMEM((n_y, n_z * OWN, LANES), BF16),
-            pltpu.VMEM((n_y, n_z * OWN, LANES), BF16),
-            pltpu.VMEM((n_z, n_y * OWN, LANES), BF16),
+            pltpu.VMEM((n_y, n_z, OWN, LANES), BF16),
+            pltpu.VMEM((n_y, n_z, OWN, LANES), BF16),
             pltpu.VMEM(block, BF16),
             pltpu.VMEM(block, BF16),
-            pltpu.VMEM((n_z, n_y * OWN, LANES), BF16),
+            pltpu.VMEM((n_z, n_y, OWN, LANES), BF16),
             pltpu.VMEM((2, 256, LANES), F32),
             pltpu.VMEM((2, 256, LANES), F32),
             pltpu.VMEM((n_dp * OWN, LANES), F32),
             pltpu.VMEM((OWN, 8 * HOP, SPAN), BF16),
             pltpu.VMEM((OWN, SPAN, SPAN), BF16),
+            pltpu.VMEM((OWN, SPAN, SPAN), BF16),
             pltpu.VMEM((OWN * HOP, SPAN), F32),
-            pltpu.VMEM((2, 256, LANES), F32),
-            pltpu.VMEM(block, BF16),
+            pltpu.VMEM((2, 2, 128, LANES), F32),
+            pltpu.VMEM((8, 2, 16, 256), BF16),
             pltpu.VMEM((OWN * HOP, SPAN), F32),
-            pltpu.VMEM((8 * HOP, SPAN), BF16),
+            pltpu.VMEM((OWN, 8 * HOP, SPAN), BF16),
+            pltpu.VMEM((OWN, 4, 8 * HOP, LANES), F32),
             pltpu.VMEM((n_dp * OWN, LANES), F32),
             pltpu.VMEM(filters.shape, BF16),
         ]
+        + [pltpu.SemaphoreType.REGULAR] * 2
         + [pltpu.SemaphoreType.DMA((5,))]
-        + [pltpu.SemaphoreType.DMA] * 12,
+        + [pltpu.SemaphoreType.DMA, pltpu.SemaphoreType.DMA((2,))]
+        + [pltpu.SemaphoreType.DMA] * 10,
         compiler_params=pltpu.CompilerParams(collective_id=0, has_side_effects=True, vmem_limit_bytes=grant),
     )(
         upstream.reshape(rows, width),

time: 34.3 us -> 33.7 us (0.983)
  Pallas kernels: 33.5 us -> 32.9 us
    pallas_call x1, Pallas kernels: 32.7 us -> 32.1 us  [body(): pl.pallas_call(functools.partial(kernel, n_ctx, n_dp, n_y), out_shape=(pl...]
where the time goes in v4:
time: 33.7 us; the launch traced here: 33.6 us
  Pallas kernels  32.9 us (98%)
  between operations  0.64 us (2%)
    pallas_call x1, Pallas kernels, body(): pl.pallas_call(functools.partial(kernel, n_ctx, n_dp, n_y), out_shape=(pl...  32.1 us
    pallas_call x1, Pallas kernels, body(): pl.pallas_call(finish_kernel, out_shape=(jax.ShapeDtypeStruct((rows, widt...  0.79 us

profile of v4, /device:TPU:1, one launch (start us, length us, event | category | flops | bytes accessed | tf_op | source)
XLA Modules:
  0.0 33.6 jit_solution(139820609513894625)
XLA Ops:
  0.6 32.1 %shard_map.68 = (bf16[16,16,256]{2,1,0:T(8,128)(2,1)S(1)}, bf16[32,8,128]{2,1,0:T(8,128)(2,1)S(1)}) custom-call(bf16[512,128]{1,0:T(8,128)(2,1)} %bitcast.4, bf16[512,128]{1,0:T(8,128)(2,1)} %bitcast.5, bf16[512,128]{1,0:T(8,128)(2,1)} %bitcast.6, f32[32,8,128]{2,1,0:T(8,128)} %filt_ref.1, f32[128]{0:T(128)} %gain_ref.1), custom_call_target="tpu_custom_call" | custom-call | tf_op jit(solution)/shard_map/pallas_call | solution.py:483
  32.8 0.8 %shard_map.69 = (bf16[512,128]{1,0:T(8,128)(2,1)}, f32[32,8,128]{2,1,0:T(8,128)}) custom-call(bf16[16,16,256]{2,1,0:T(8,128)(2,1)S(1)} %get-tuple-element.6.y_in, bf16[32,8,128]{2,1,0:T(8,128)(2,1)S(1)} %get-tuple-element.7.d_in), custom_call_target="tpu_custom_call" | custom-call | tf_op jit(solution)/shard_map/pallas_call | solution.py:529

commit v5 on v4

--- a/solution.py
+++ b/solution.py
@@ -16,6 +16,7 @@
 LANES = 128
 OWN = 8
 SEQ = 2
+FIRST = 1
 LINE = 8
 
 
@@ -184,6 +185,14 @@
         peer = (1 - me_hi) * half + lax.rem(me_lo + step, half)
         return peer, {"ctx": peer, "dp": me_dp}
 
+    def first_far(step):
+        peer = (1 - me_hi) * half + FIRST
+        return peer, {"ctx": peer, "dp": me_dp}
+
+    def other_far(step):
+        peer = (1 - me_hi) * half + lax.rem(FIRST + 1 + lax.rem(me_lo + step, half - 1), half)
+        return peer, {"ctx": peer, "dp": me_dp}
+
     def near_ctx(step):
         peer = me_hi * half + lax.rem(me_lo + step, half)
         return peer, {"ctx": peer, "dp": me_dp}
@@ -299,8 +308,17 @@
     loaded(1, gate)
     wide[...] = (up[...].astype(F32) * gate[...].astype(F32)).astype(BF16).astype(F32)
     spread_rows(wide, gsend)
+    loaded(2, raw)
+    wide[...] = raw[...].astype(F32)
+    spread_rows(wide, xsend)
     pl.semaphore_wait(barrier, greeted)
-    scatter(0, half, far_ctx, me_ctx, gsend, grecv, g_send_sem, g_recv_sem)
+    scatter(0, 1, first_far, me_ctx, gsend, grecv, g_send_sem, g_recv_sem)
+
+    @pl.when(me_hi == 1)
+    def _():
+        scatter(0, 1, first_far, me_ctx, xsend, xrecv, x_send_sem, x_recv_sem)
+
+    scatter(0, half - 1, other_far, me_ctx, gsend, grecv, g_send_sem, g_recv_sem)
     @pl.when(me_hi == 1)
     def _():
         for step in (2, n_y - 2):
@@ -338,13 +356,10 @@
             def _():
                 scatter(step, step + 1, over_y, me_y, hsend, hpass, h_send_sem, h_recv_sem.at[1])
 
-    loaded(2, raw)
-    wide[...] = raw[...].astype(F32)
-    spread_rows(wide, xsend)
-
-    @pl.when(me_hi == 1)
-    def _():
-        scatter(0, half, far_ctx, me_ctx, xsend, xrecv, x_send_sem, x_recv_sem)
+
+    @pl.when(me_hi == 1)
+    def _():
+        scatter(0, half - 1, other_far, me_ctx, xsend, xrecv, x_send_sem, x_recv_sem)
 
     scatter(1, half, near_ctx, me_ctx, gsend, grecv, g_send_sem, g_recv_sem)
     scatter(1, half, near_ctx, me_ctx, xsend, xrecv, x_send_sem, x_recv_sem)

time: 33.7 us -> 33.7 us (level)
  no operation moved by 1% of the time
where the time goes in v5:
time: 33.7 us; the launch traced here: 33.4 us
  Pallas kernels  32.8 us (97%)
  between operations  0.64 us (2%)
    pallas_call x1, Pallas kernels, body(): pl.pallas_call(functools.partial(kernel, n_ctx, n_dp, n_y), out_shape=(pl...  32 us
    pallas_call x1, Pallas kernels, body(): pl.pallas_call(finish_kernel, out_shape=(jax.ShapeDtypeStruct((rows, widt...  0.79 us

profile of v5, /device:TPU:1, one launch (start us, length us, event | category | flops | bytes accessed | tf_op | source)
XLA Modules:
  0.0 33.4 jit_solution(6990890538789521480)
XLA Ops:
  0.6 32.0 %shard_map.68 = (bf16[16,16,256]{2,1,0:T(8,128)(2,1)S(1)}, bf16[32,8,128]{2,1,0:T(8,128)(2,1)S(1)}) custom-call(bf16[512,128]{1,0:T(8,128)(2,1)} %bitcast.4, bf16[512,128]{1,0:T(8,128)(2,1)} %bitcast.5, bf16[512,128]{1,0:T(8,128)(2,1)} %bitcast.6, f32[32,8,128]{2,1,0:T(8,128)} %filt_ref.1, f32[128]{0:T(128)} %gain_ref.1), custom_call_target="tpu_custom_call" | custom-call | tf_op jit(solution)/shard_map/pallas_call | solution.py:498
  32.6 0.8 %shard_map.69 = (bf16[512,128]{1,0:T(8,128)(2,1)}, f32[32,8,128]{2,1,0:T(8,128)}) custom-call(bf16[16,16,256]{2,1,0:T(8,128)(2,1)S(1)} %get-tuple-element.6.y_in, bf16[32,8,128]{2,1,0:T(8,128)(2,1)S(1)} %get-tuple-element.7.d_in), custom_call_target="tpu_custom_call" | custom-call | tf_op jit(solution)/shard_map/pallas_call | solution.py:544

commit v6 on v5

--- a/solution.py
+++ b/solution.py
@@ -411,7 +411,7 @@
             for c in range(OWN):
                 build_toeplitz(hwide, toep, c)
 
-            for h in range(2):
+            for h in (1, 0):
                 for c in range(OWN):
                     back_rows(toep, wint, yall, c, h)
                 finish_back(yall, gwide, gain, me_ctx * OWN, ywide.at[h], ysend, h)

time: 33.7 us -> 33.4 us (level)
    pallas_call x1, Pallas kernels: 32 us -> 31.7 us  [body(): pl.pallas_call(functools.partial(kernel, n_ctx, n_dp, n_y), out_shape=(pl...]
where the time goes in v6:
time: 33.4 us; the launch traced here: 33.1 us
  Pallas kernels  32.5 us (97%)
  between operations  0.64 us (2%)
    pallas_call x1, Pallas kernels, body(): pl.pallas_call(functools.partial(kernel, n_ctx, n_dp, n_y), out_shape=(pl...  31.7 us
    pallas_call x1, Pallas kernels, body(): pl.pallas_call(finish_kernel, out_shape=(jax.ShapeDtypeStruct((rows, widt...  0.79 us

profile of v6, /device:TPU:1, one launch (start us, length us, event | category | flops | bytes accessed | tf_op | source)
XLA Modules:
  0.0 33.1 jit_solution(6286388207165606362)
XLA Ops:
  0.6 31.7 %shard_map.68 = (bf16[16,16,256]{2,1,0:T(8,128)(2,1)S(1)}, bf16[32,8,128]{2,1,0:T(8,128)(2,1)S(1)}) custom-call(bf16[512,128]{1,0:T(8,128)(2,1)} %bitcast.4, bf16[512,128]{1,0:T(8,128)(2,1)} %bitcast.5, bf16[512,128]{1,0:T(8,128)(2,1)} %bitcast.6, f32[32,8,128]{2,1,0:T(8,128)} %filt_ref.1, f32[128]{0:T(128)} %gain_ref.1), custom_call_target="tpu_custom_call" | custom-call | tf_op jit(solution)/shard_map/pallas_call | solution.py:498
  32.3 0.8 %shard_map.69 = (bf16[512,128]{1,0:T(8,128)(2,1)}, f32[32,8,128]{2,1,0:T(8,128)}) custom-call(bf16[16,16,256]{2,1,0:T(8,128)(2,1)S(1)} %get-tuple-element.6.y_in, bf16[32,8,128]{2,1,0:T(8,128)(2,1)S(1)} %get-tuple-element.7.d_in), custom_call_target="tpu_custom_call" | custom-call | tf_op jit(solution)/shard_map/pallas_call | solution.py:544

commit v7 on v6

--- a/solution.py
+++ b/solution.py
@@ -418,7 +418,7 @@
 
                 @pl.loop(0, n_ctx // 2)
                 def _(step):
-                    block = half // 2 * (step // (half // 2)) + lax.rem(me_lo // 2 + step, half // 2)
+                    block = step
                     peer = 2 * block + h
 
                     @pl.when(peer != me_ctx)

time: 33.4 us -> 33.4 us (level)
  no operation moved by 1% of the time
where the time goes in v7:
time: 33.4 us; the launch traced here: 33 us
  Pallas kernels  32.3 us (97%)
  between operations  0.64 us (2%)
    pallas_call x1, Pallas kernels, body(): pl.pallas_call(functools.partial(kernel, n_ctx, n_dp, n_y), out_shape=(pl...  31.5 us
    pallas_call x1, Pallas kernels, body(): pl.pallas_call(finish_kernel, out_shape=(jax.ShapeDtypeStruct((rows, widt...  0.79 us

profile of v7, /device:TPU:1, one launch (start us, length us, event | category | flops | bytes accessed | tf_op | source)
XLA Modules:
  0.0 33.0 jit_solution(14601335484696162897)
XLA Ops:
  0.6 31.5 %shard_map.68 = (bf16[16,16,256]{2,1,0:T(8,128)(2,1)S(1)}, bf16[32,8,128]{2,1,0:T(8,128)(2,1)S(1)}) custom-call(bf16[512,128]{1,0:T(8,128)(2,1)} %bitcast.4, bf16[512,128]{1,0:T(8,128)(2,1)} %bitcast.5, bf16[512,128]{1,0:T(8,128)(2,1)} %bitcast.6, f32[32,8,128]{2,1,0:T(8,128)} %filt_ref.1, f32[128]{0:T(128)} %gain_ref.1), custom_call_target="tpu_custom_call" | custom-call | tf_op jit(solution)/shard_map/pallas_call | solution.py:498
  32.2 0.8 %shard_map.69 = (bf16[512,128]{1,0:T(8,128)(2,1)}, f32[32,8,128]{2,1,0:T(8,128)}) custom-call(bf16[16,16,256]{2,1,0:T(8,128)(2,1)S(1)} %get-tuple-element.6.y_in, bf16[32,8,128]{2,1,0:T(8,128)(2,1)S(1)} %get-tuple-element.7.d_in), custom_call_target="tpu_custom_call" | custom-call | tf_op jit(solution)/shard_map/pallas_call | solution.py:544
